TPU v7x, 32 devices: a whole 2x2x4 slice. The times are simulated.
32 devices in a mesh: var: 8 (over y, x, core), space: 4 (over z).
Axes of the slice: x: 2, y: 2, z: 4, core: 2. Of those that a mesh axis runs over, the one named last changes fastest.
Arguments:
- patches: bfloat16 [48, 1024, 256], P('var', 'space'), may hold values from -6 to 6
- embed_weight: bfloat16 [48, 256, 1024], P('var'), may hold values from -0.375 to 0.375
- var_embed: float32 [48, 1024], P('var'), may hold values from -3 to 3
- agg_query: float32 [1024], replicated, may hold values from -240 to 240
- agg_kv: bfloat16 [1024, 2048], replicated, may hold values from -0.1875 to 0.1875
- agg_out: bfloat16 [1024, 1024], replicated, may hold values from -0.1875 to 0.1875
- norm_gain: float32 [1024], replicated, may hold values from 0.5 to 1.5
- qkv_weight: bfloat16 [1024, 3072], P(None, 'var'), may hold values from -4 to 4
- out_weight: bfloat16 [1024, 1024], P('var'), may hold values from -0.1875 to 0.1875
- cotangent: bfloat16 [1024, 1024], P('space'), may hold values from -6 to 6
Outputs:
- grad_embed: float32 [48, 256, 1024], P('var', None, 'space')
- grad_var_embed: float32 [48, 1024], P('var', 'space')
- grad_agg_query: float32 [1024], P('space')
- grad_agg_kv: float32 [1024, 2048], P(None, 'space')
- grad_agg_out: float32 [1024, 1024], P(None, 'space')
- grad_norm_gain: float32 [1024], P('space')
- grad_qkv: float32 [1024, 3072], P('space', 'var')
- grad_out_weight: float32 [1024, 1024], P('var', 'space')
All inputs are finite; a program needn't handle non-finite values.
Results may differ from a plain program's by a relative error of at most 0.019.
The roundings to bfloat16 on the way count: a program that leaves them out, or rounds other values in their place, can miss the bound.
Values may be sent and summed in bfloat16 or wider, within the bound.
No kernel may reach another device: no remote copies, remote signals or barrier semaphores. Data moves between devices by JAX's collectives and lax.ppermute only.
A program may use at most 128 MiB of HBM per device.

v0:
```python
import functools
import math

import jax
import jax.numpy as jnp
from jax import lax
from jax.experimental import pallas as pl
from jax.experimental.pallas import tpu as pltpu
from jax.sharding import PartitionSpec as P

HEADS = 16
LANES = 128
EPSILON = 1e-05
MIB = 1 << 20

LIMITS = {
    "early": 60, "forward": 24, "columns": 8, "pool_pair": 16, "pool": 16, "norm": 16, "attention": 24,
    "dn": 12, "dn_pair": 16, "joined": 16, "prepare": 16, "out_grad": 16, "dvalue": 24, "embed": 24, "value_grad": 32,
    "add": 12, "pair_sum": 16, "packet_split": 16, "space_sum": 16, "head_grads": 16, "final": 16, "embed_final": 24,
}

F32 = jnp.float32
BF16 = jnp.bfloat16

NN = (((1,), (0,)), ((), ()))
NT = (((1,), (1,)), ((), ()))
TN = (((0,), (0,)), ((), ()))


def mm(a, b, dims=NN):
    return lax.dot_general(a, b, dims, preferred_element_type=F32)


def iota(shape, axis):
    return lax.broadcasted_iota(jnp.int32, shape, axis)


def parts3(x):
    hi = x.astype(BF16).astype(F32)
    rest = x - hi
    mid = rest.astype(BF16).astype(F32)
    return hi, mid, rest - mid


def pack(x, y=None):
    group = iota(x.shape, 1) >> 4
    hi, mid, lo = parts3(x)
    out = jnp.where(group == 0, hi, jnp.where(group == 1, mid, jnp.where(group == 2, lo, 0.0)))
    if y is not None:
        hi, mid, lo = parts3(y)
        out = jnp.where(group == 3, hi, jnp.where(group == 4, mid, jnp.where(group == 5, lo, out)))
    return out.astype(BF16)


def unpack(packed, first_group=0):
    row, column = iota((LANES, LANES), 0), iota((LANES, LANES), 1)
    group = row >> 4
    take = ((row & 15) == (column & 15)) & (group >= first_group) & (group < first_group + 3)
    return mm(packed, jnp.where(take, 1.0, 0.0).astype(BF16))


def spread_matrix(width, size, first=0):
    row, column = iota((LANES, width), 0), iota((LANES, width), 1)
    shift = size.bit_length() - 1
    take = ((row & 15) == ((column + first) >> shift)) & (row < 48)
    return jnp.where(take, 1.0, 0.0).astype(BF16)


def fold_matrix(width, size):
    row, column = iota((width, LANES), 0), iota((width, LANES), 1)
    shift = size.bit_length() - 1
    return jnp.where((column & 15) == (row >> shift), 1.0, 0.0).astype(BF16)


def head_sums(x, fold):
    hi, mid, lo = parts3(x)
    return mm(hi.astype(BF16), fold) + mm(mid.astype(BF16), fold) + mm(lo.astype(BF16), fold)


def call(body, out_shape, limit=16, after=(), in_specs=None, **kw):
    def run(*args):
        n, m = len(args), len(after)
        vmem = pl.BlockSpec(memory_space=pltpu.VMEM)
        return pl.pallas_call(
            lambda *refs: body(*refs[:n], *refs[n + m :]),
            out_shape=out_shape,
            in_specs=([vmem] * n if in_specs is None else list(in_specs)) + [vmem] * m,
            compiler_params=pltpu.CompilerParams(vmem_limit_bytes=limit * MIB),
            **kw,
        )(*args, *after)

    return run


def struct(shape, dtype):
    return jax.ShapeDtypeStruct(shape, dtype)


def cost(flops, moved):
    return pl.CostEstimate(flops=int(flops), bytes_accessed=int(moved), transcendentals=0)


SMEM = pl.BlockSpec(memory_space=pltpu.SMEM)


def swap(x, axis, k, keep=None):
    pairs = [(i, i ^ k) for i in range(lax.axis_size(axis))]
    if keep is not None:
        pairs = [pair for pair in pairs if keep(pair[1])]
    return lax.ppermute(x, axis, pairs)


def gather_direct(x, axis):
    return [x] + [swap(x, axis, k) for k in range(1, lax.axis_size(axis))]


def exchange_direct(blocks, axis):
    return [blocks[0]] + [swap(blocks[k], axis, k) for k in range(1, len(blocks))]


def gather_pairs(x, axis, stack=jnp.stack):
    even = [x] + [swap(x, axis, k) for k in range(2, lax.axis_size(axis), 2)]
    even = stack(even)
    return even, swap(even, axis, 1)


def exchange_pairs(keep, send, combine):
    parts = combine(keep, swap(send, "var", 1))
    return [parts[0]] + [swap(parts[k], "var", 2 * k) for k in range(1, len(parts))]


def pair_rows(me_v, k, odd, block):
    device = (((me_v >> 1) ^ k) << 1) + ((me_v & 1) ^ odd)
    return pl.ds(pl.multiple_of(device * block, block), block)


def three_rows(x):
    hi, mid, lo = parts3(x)
    row = iota((16, x.shape[1]), 0)
    return jnp.where(row == 0, hi, jnp.where(row == 1, mid, jnp.where(row == 2, lo, 0.0))).astype(BF16)


def head_order(width, size=64):
    heads = width // (3 * size)
    row, column = iota((width, width), 0), iota((width, width), 1)
    take = jnp.zeros((width, width), jnp.bool_)
    for h in range(heads):
        for c in range(3):
            start, target = h * 3 * size + c * size, c * heads * size + h * size
            inside = (column >= target) & (column < target + size)
            take = take | (inside & ((row - start) == (column - target)))
    return jnp.where(take, 1.0, 0.0).astype(BF16)


def early_body(me_ref, cot_ref, outw_ref, qkvw_ref, dattn_ref, own_ref, wperm_ref):
    dattn_ref[...] = mm(cot_ref[...], outw_ref[...], NT).astype(BF16)
    block = own_ref.shape[0]
    own_ref[...] = cot_ref[pl.ds(pl.multiple_of(me_ref[0] * block, block), block), :]
    wperm_ref[...] = mm(qkvw_ref[...], head_order(qkvw_ref.shape[1])).astype(BF16)


def forward_part(start, patches_ref, embed_ref, offset_ref, wq, wv_ref, spread, outs, state):
    tokens_ref, value_ref, scores_ref = outs
    here = tokens_ref.shape[0]
    width = tokens_ref.shape[2]
    for v in range(here):
        u = start + v
        tokens = (mm(patches_ref[u], embed_ref[u]) + offset_ref[u : u + 1, :]).astype(BF16)
        tokens_ref[v] = tokens
        pieces = mm(tokens, wq)
        scores_ref[v] = pieces[:, :LANES] + pieces[:, LANES : 2 * LANES] + pieces[:, 2 * LANES :]
        value_ref[v] = mm(tokens, wv_ref[:, width:])
    top = functools.reduce(jnp.maximum, [scores_ref[v] for v in range(here)])
    total, acc = 0.0, 0.0
    if state is not None:
        top = jnp.maximum(top, state[0])
        old = jnp.exp(state[0] - top)
        total, acc = state[1] * old, state[2] * mm(pack(old), spread)
    for v in range(here):
        new = jnp.exp(scores_ref[v] - top)
        total = total + new
        acc = acc + value_ref[v] * mm(pack(new), spread)
    return top, total, acc


def first_body(
    scale, patches_ref, embed_ref, offset_ref, query_ref, kv_ref,
    tokens_ref, value_ref, scores_ref, wq_ref, wback_ref, acc_ref, max_ref, sum_ref,
):
    width = tokens_ref.shape[2]
    size = width // HEADS
    row, column = iota((LANES, width), 0), iota((LANES, width), 1)
    own = (row & 15) == (column >> (size.bit_length() - 1))
    wq = jnp.zeros((width, LANES), F32)
    for part in parts3(query_ref[...]):
        wq = wq + mm(kv_ref[:, :width], jnp.where(own, part, 0.0).astype(BF16), NT)
    hi, mid, lo = parts3(wq * scale)
    wq_ref[:, :LANES] = hi.astype(BF16)
    wq_ref[:, LANES : 2 * LANES] = mid.astype(BF16)
    wq_ref[:, 2 * LANES :] = lo.astype(BF16)
    group = iota((width, LANES), 1) >> 4
    back = jnp.where((group == 0) | (group == 2), hi, jnp.where(group == 1, mid, 0.0))
    wback_ref[...] = back.astype(BF16)
    max_ref[...], sum_ref[...], acc_ref[...] = forward_part(
        0, patches_ref, embed_ref, offset_ref, wq_ref[...], kv_ref, spread_matrix(width, size),
        (tokens_ref, value_ref, scores_ref), None,
    )


def second_body(
    start, me_ref, patches_ref, embed_ref, offset_ref, wq_ref, kv_ref, acc0_ref, max0_ref, sum0_ref,
    tokens_ref, value_ref, scores_ref, keep_ref, send_ref, acc_ref, max_ref,
):
    width = tokens_ref.shape[2]
    top, total, acc = forward_part(
        start, patches_ref, embed_ref, offset_ref, wq_ref[...], kv_ref, spread_matrix(width, width // HEADS),
        (tokens_ref, value_ref, scores_ref), (max0_ref[...], sum0_ref[...], acc0_ref[...]),
    )
    acc_ref[...] = acc
    max_ref[...] = jnp.where(iota(top.shape, 1) < LANES // 2, top, total)
    block = keep_ref.shape[1]
    core = me_ref[0] & 1
    for c in range(keep_ref.shape[0]):
        for ref, device in ((keep_ref, 2 * c + core), (send_ref, 2 * c + 1 - core)):
            at = pl.ds(pl.multiple_of(device * block, block), block)
            ref[c, :, :width] = acc_ref[at, :]
            ref[c, :, width:] = max_ref[at, :]


def halves_of(both):
    low = iota(both.shape, 1) < LANES // 2
    turned = pltpu.roll(both, LANES // 2, 1)
    return jnp.where(low, both, turned), jnp.where(low, turned, both)


def pool_pair_body(me_ref, keep_ref, got_ref, *out_refs):
    width = keep_ref.shape[2] - LANES
    spread = spread_matrix(width, width // HEADS)
    low = iota((keep_ref.shape[1], LANES), 1) < LANES // 2
    for k, out_ref in enumerate(out_refs):
        slot = (me_ref[0] >> 1) ^ k
        mine, other = keep_ref[slot], got_ref[slot]
        max_a, sum_a = halves_of(mine[:, width:])
        max_b, sum_b = halves_of(other[:, width:])
        top = jnp.maximum(max_a, max_b)
        factor_a, factor_b = jnp.exp(max_a - top), jnp.exp(max_b - top)
        out_ref[:, :width] = mine[:, :width] * mm(pack(factor_a), spread) + other[:, :width] * mm(pack(factor_b), spread)
        out_ref[:, width:] = jnp.where(low, top, sum_a * factor_a + sum_b * factor_b)


def pool_body(n, *refs):
    ins, (mixed_ref, packet_ref) = refs[:n], refs[n:]
    width = mixed_ref.shape[1]
    stats = [halves_of(ref[:, width:]) for ref in ins]
    top = functools.reduce(jnp.maximum, [m for m, _ in stats])
    factors = [jnp.exp(m - top) for m, _ in stats]
    total = sum(s * f for (_, s), f in zip(stats, factors))
    spread = spread_matrix(width, width // HEADS)
    mixed = jnp.zeros(mixed_ref.shape, F32)
    for ref, factor in zip(ins, factors):
        mixed = mixed + ref[:, :width] * mm(pack(factor / total), spread)
    mixed_ref[...] = mixed
    packet_ref[:, :width] = mixed.astype(BF16)
    packet_ref[:, width:] = pack(top, total)


def norm_body(
    me_ref, even_ref, odd_ref, agg_ref, gain_ref, w_ref, qkv_ref, normed_ref, packets_ref, centred_ref, inv_ref,
    all_ref, allinv_ref,
):
    width = agg_ref.shape[0]
    block = centred_ref.shape[0]
    for k in range(even_ref.shape[0]):
        for odd, ref in ((0, even_ref), (1, odd_ref)):
            packets_ref[pair_rows(me_ref[0], k, odd, block), :] = ref[k]
    joined = mm(packets_ref[:, :width], agg_ref[...]).astype(BF16).astype(F32)
    mean = jnp.mean(joined, axis=-1, keepdims=True)
    spread_sq = jnp.mean((joined - mean) ** 2, axis=-1, keepdims=True)
    inv = lax.rsqrt(spread_sq + EPSILON)
    centred = (joined - mean) * inv
    normed = (centred * gain_ref[...]).astype(BF16)
    qkv_ref[...] = mm(normed, w_ref[...]).astype(BF16)
    normed_ref[...] = normed
    all_ref[...] = centred
    allinv_ref[...] = jnp.broadcast_to(inv, allinv_ref.shape)
    start = pl.multiple_of(me_ref[0] * block, block)
    centred_ref[...] = all_ref[pl.ds(start, block), :]
    inv_ref[...] = allinv_ref[pl.ds(start, block), :]


def attention_body(n_space, size, scale, *refs):
    qkv_refs, dattn_refs = refs[:n_space], refs[n_space : 2 * n_space]
    attn_ref, dqkv_ref, k_ref, v_ref, dk_ref, dv_ref = refs[2 * n_space :]
    rows, group = dattn_refs[0].shape
    heads = group // size
    for b in range(n_space):
        at = slice(b * rows, (b + 1) * rows)
        k_ref[at, :] = qkv_refs[b][:, group : 2 * group]
        v_ref[at, :] = qkv_refs[b][:, 2 * group :]
    lane_head = iota((rows, group), 1) // size if heads > 1 else None
    for b in range(n_space):
        at = slice(b * rows, (b + 1) * rows)
        queries, d_out = qkv_refs[b][:, :group], dattn_refs[b][...]
        attn = dq = None
        for h in range(heads):
            if heads > 1:
                q_h = jnp.where(lane_head == h, queries.astype(F32), 0.0).astype(BF16)
                do_h = jnp.where(lane_head == h, d_out.astype(F32), 0.0).astype(BF16)
            else:
                q_h, do_h = queries, d_out
            logits = mm((q_h.astype(F32) * scale).astype(BF16), k_ref[...], NT)
            shifted = jnp.exp(logits - jnp.max(logits, axis=-1, keepdims=True))
            probs = shifted * (1.0 / jnp.sum(shifted, axis=-1, keepdims=True))
            probs_b = probs.astype(BF16)
            attn_h = mm(probs_b, v_ref[...])
            dprob = mm((do_h.astype(F32) * scale).astype(BF16), v_ref[...], NT)
            delta = jnp.sum(probs * dprob, axis=-1, keepdims=True)
            dscore = (probs * (dprob - delta)).astype(BF16)
            dq_h = mm(dscore, k_ref[...])
            dk = mm(dscore, q_h, TN)
            dv = mm(probs_b, do_h, TN)
            if b == 0 and h == 0:
                dk_ref[...] = dk
                dv_ref[...] = dv
            else:
                dk_ref[...] += dk
                dv_ref[...] += dv
            attn = attn_h if attn is None else jnp.where(lane_head == h, attn_h, attn)
            dq = dq_h if dq is None else jnp.where(lane_head == h, dq_h, dq)
        attn_ref[at, :] = attn.astype(BF16)
        dqkv_ref[at, :group] = dq.astype(BF16)
    dqkv_ref[:, group : 2 * group] = dk_ref[...].astype(BF16)
    dqkv_ref[:, 2 * group :] = dv_ref[...].astype(BF16)


def dn_body(me_ref, dqkv_ref, w_ref, keep_ref, send_ref, dn_ref):
    dn_ref[...] = mm(dqkv_ref[...], w_ref[...], NT).astype(BF16)
    block = keep_ref.shape[1]
    core = me_ref[0] & 1
    for c in range(keep_ref.shape[0]):
        for ref, device in ((keep_ref, 2 * c + core), (send_ref, 2 * c + 1 - core)):
            ref[c] = dn_ref[pl.ds(pl.multiple_of(device * block, block), block), :]


def columns_body(n_space, me_ref, in_ref, *refs):
    out_refs, (cols_ref,) = refs[:n_space], refs[n_space:]
    cols = cols_ref.shape[2]
    for c in range(n_space):
        cols_ref[c] = in_ref[:, c * cols : (c + 1) * cols]
    for k in range(n_space):
        out_refs[k][...] = cols_ref[me_ref[1] ^ k]


def head_grads_body(n_space, *refs):
    normed_refs, (dqkv_ref, gqkv_ref, flag_ref) = refs[:n_space], refs[n_space:]
    flag_ref[...] = jnp.zeros(flag_ref.shape, F32)
    rows = normed_refs[0].shape[0]
    natural = mm(dqkv_ref[...], head_order(dqkv_ref.shape[1]), NT).astype(BF16)
    gqkv_ref[...] = sum(
        mm(ref[...], natural[b * rows : (b + 1) * rows, :], TN) for b, ref in enumerate(normed_refs)
    )


def dn_pair_body(me_ref, keep_ref, got_ref, *out_refs):
    for k, out_ref in enumerate(out_refs):
        slot = (me_ref[0] >> 1) ^ k
        out_ref[...] = (keep_ref[slot].astype(F32) + got_ref[slot].astype(F32)).astype(BF16)


def joined_body(n, *refs):
    ins = refs[:n]
    centred_ref, inv_ref, gain_ref, cot_ref, mixed_ref, agg_ref, packet_ref, dgain_ref = refs[n:]
    width = centred_ref.shape[1]
    d_normed = sum(ref[...].astype(F32) for ref in ins)
    centred = centred_ref[...]
    dgain_ref[...] = jnp.broadcast_to(jnp.sum(d_normed * centred, axis=0, keepdims=True), dgain_ref.shape)
    gained = d_normed * gain_ref[...]
    inner = (
        gained
        - jnp.mean(gained, axis=-1, keepdims=True)
        - centred * jnp.mean(gained * centred, axis=-1, keepdims=True)
    )
    d_joined = (cot_ref[...].astype(F32) + inner * inv_ref[:, :1]).astype(BF16)
    d_pooled = mm(d_joined, agg_ref[...], NT)
    center = pack(head_sums(d_pooled * mixed_ref[...], fold_matrix(width, width // HEADS)))
    packet_ref[:, :width] = d_joined
    packet_ref[:, width:] = center


def prepare_body(me_ref, pooled_ref, even_ref, odd_ref, agg_ref, djoined_ref, dpool_ref, stat_ref):
    width = agg_ref.shape[0]
    for k in range(even_ref.shape[0]):
        for odd, ref in ((0, even_ref), (1, odd_ref)):
            djoined_ref[pair_rows(me_ref[0], k, odd, even_ref.shape[1]), :] = ref[k]
    dpool_ref[...] = mm(djoined_ref[:, :width], agg_ref[...], NT)
    stat_ref[0] = unpack(djoined_ref[:, width:])
    stat_ref[1] = unpack(pooled_ref[:, width:])
    stat_ref[2] = 1.0 / unpack(pooled_ref[:, width:], 3)


def out_grad_body(me_ref, pooled_ref, djoined_ref, dgain_ref, attn_ref, cot_ref, keep_ref, send_ref, all_ref, cols_ref):
    width = dgain_ref.shape[1]
    all_ref[...] = mm(pooled_ref[:, :width], djoined_ref[:, :width], TN)
    weight_grad = mm(attn_ref[...], cot_ref[...], TN).astype(BF16)
    n_space, height, cols = cols_ref.shape
    block = height - 16 - weight_grad.shape[0]
    start = pl.multiple_of(me_ref[0] * block, block)
    own = all_ref[pl.ds(start, block), :].astype(BF16)
    extra = three_rows(dgain_ref[:1, :])
    for c in range(n_space):
        cols_ref[c, :block, :] = own[:, c * cols : (c + 1) * cols]
        cols_ref[c, block : block + 16, :] = extra[:, c * cols : (c + 1) * cols]
        cols_ref[c, block + 16 :, :] = weight_grad[:, c * cols : (c + 1) * cols]
    for k in range(n_space):
        (send_ref if k % 2 else keep_ref)[k // 2] = cols_ref[me_ref[1] ^ k]


def out_add_body(block, mine_ref, got_ref, *refs):
    for j, out_ref in enumerate(refs):
        total = mine_ref[j + 1].astype(F32) + got_ref[j + 1].astype(F32)
        out_ref[...] = total.astype(BF16)
        out_ref[block : block + 16, :] = three_rows(jnp.sum(total[block : block + 16, :], axis=0, keepdims=True))


def dvalue_body(dpool_ref, stat_ref, value_ref, scores_ref, dvalue_ref, dlogit_ref, spread_ref, fold_ref):
    width = dpool_ref.shape[1]
    size = width // HEADS

    @pl.when(pl.program_id(0) == 0)
    def _():
        spread_ref[...] = spread_matrix(width, size)
        fold_ref[...] = fold_matrix(width, size)

    weight = jnp.exp(scores_ref[0] - stat_ref[1]) * stat_ref[2]
    dvalue_ref[0] = (mm(pack(weight), spread_ref[...]) * dpool_ref[...]).astype(BF16)
    dweight = head_sums(dpool_ref[...] * value_ref[0], fold_ref[...])
    dlogit = weight * (dweight - stat_ref[0])
    hi = dlogit.astype(BF16)
    dlogit_ref[0, :, :LANES] = hi
    dlogit_ref[0, :, LANES:] = (dlogit - hi.astype(F32)).astype(BF16)


def embed_body(
    n_space, me_ref, dvalue_ref, dlogit_ref, patches_ref, wv_ref, wback_ref, keep_ref, send_ref, cols_ref, extra_ref
):
    v = pl.program_id(0)
    hi, lo = dlogit_ref[0, :, :LANES].astype(F32), dlogit_ref[0, :, LANES:].astype(F32)
    group = iota(hi.shape, 1) >> 4
    mixed = jnp.where(group < 2, hi, jnp.where(group == 2, lo, 0.0)).astype(BF16)
    d_tokens = (mm(dvalue_ref[0], wv_ref[...], NT) + mm(mixed, wback_ref[...], NT)).astype(BF16)
    grad = mm(patches_ref[0], d_tokens, TN).astype(BF16)
    hi, lo, _ = parts3(jnp.sum(d_tokens.astype(F32), axis=0, keepdims=True))
    row = iota(extra_ref.shape, 0)
    extra = jnp.where(row == 2 * v, hi, jnp.where(row == 2 * v + 1, lo, 0.0))

    @pl.when(v == 0)
    def _():
        extra_ref[...] = extra

    @pl.when(v > 0)
    def _():
        extra_ref[...] += extra

    cols = cols_ref.shape[2]
    pixels = patches_ref.shape[2]
    for c in range(n_space):
        cols_ref[c] = grad[:, c * cols : (c + 1) * cols]
    at = pl.ds(pl.multiple_of(v * pixels, pixels), pixels)
    for k in range(0, n_space, 2):
        keep_ref[k // 2, at, :] = cols_ref[me_ref[1] ^ k]
        send_ref[k // 2, at, :] = cols_ref[me_ref[1] ^ (k + 1)]

    @pl.when(v == pl.num_programs(0) - 1)
    def _():
        tail = slice(keep_ref.shape[1] - 16, keep_ref.shape[1])
        for c in range(n_space):
            cols_ref[c, :16, :] = extra_ref[:, c * cols : (c + 1) * cols].astype(BF16)
        for k in range(0, n_space, 2):
            keep_ref[k // 2, tail, :] = cols_ref[me_ref[1] ^ k, :16, :]
            send_ref[k // 2, tail, :] = cols_ref[me_ref[1] ^ (k + 1), :16, :]


def embed_final_body(parts, *refs):
    ins, (grad_ref, offset_ref) = refs[:-2], refs[-2:]
    pixels = grad_ref.shape[1]
    base = 0
    for chunk in range(len(ins) // parts):
        total = 0.0
        for ref in ins[chunk * parts : (chunk + 1) * parts]:
            total = total + (ref[0] if len(ref.shape) == 3 else ref[...]).astype(F32)
        count = (total.shape[0] - 16) // pixels
        for v in range(count):
            grad_ref[base + v] = total[v * pixels : (v + 1) * pixels, :]
            row = count * pixels + 2 * v
            offset_ref[base + v : base + v + 1, :] = total[row : row + 1, :] + total[row + 1 : row + 2, :]
        base += count


def stack_body(*refs):
    for k, ref in enumerate(refs[:-1]):
        refs[-1][k] = ref[...]


def value_grad_body(me_ref, *refs):
    tokens_refs, dv_refs, dl_refs, (keep_ref, send_ref, all_ref) = refs[:2], refs[2:4], refs[4:6], refs[6:]
    width = dv_refs[0].shape[2]
    total, both = 0.0, 0.0
    for tokens_ref, dv_ref, dl_ref in zip(tokens_refs, dv_refs, dl_refs):
        for v in range(dv_ref.shape[0]):
            total = total + mm(tokens_ref[v], dv_ref[v], TN)
            both = both + mm(tokens_ref[v], dl_ref[v], TN)
    all_ref[:, :width] = total.astype(BF16)
    all_ref[:, width:] = pack(both[:, :LANES] + both[:, LANES:])
    block = keep_ref.shape[1]
    count = all_ref.shape[0] // block
    for r in range(count):
        target = pl.program_id(0) * count + r
        same = (target & 1) == (me_ref[0] & 1)
        slot = target >> 1

        @pl.when(same)
        def _():
            keep_ref[slot] = all_ref[r * block : (r + 1) * block, :]

        @pl.when(jnp.logical_not(same))
        def _():
            send_ref[slot] = all_ref[r * block : (r + 1) * block, :]


def pair_sum_body(n_chip, me_ref, keep_ref, got_ref, *out_refs):
    width = keep_ref.shape[2] - LANES
    for k in range(n_chip):
        slot = (me_ref[0] >> 1) ^ k
        mine, other = keep_ref[slot], got_ref[slot]
        out_refs[k][:, :width] = (mine[:, :width].astype(F32) + other[:, :width].astype(F32)).astype(BF16)
        out_refs[k][:, width:] = pack(unpack(mine[:, width:]) + unpack(other[:, width:]))


def packet_split_body(n_in, n_space, me_ref, *refs):
    ins, out_refs, (cols_ref,) = refs[:n_in], refs[n_in:-1], refs[-1:]
    block, width = ins[0].shape[0], ins[0].shape[1] - LANES
    total = sum(ref[:, :width].astype(F32) for ref in ins).astype(BF16)
    factor = pack(sum(unpack(ref[:, width:]) for ref in ins))
    half = n_space // 2
    cols = cols_ref.shape[2] // 2
    for c in range(half):
        cols_ref[c] = total[:, 2 * c * cols : 2 * (c + 1) * cols]
    part = out_refs[0].shape[0] - 2 * block
    for k in range(n_space):
        for piece in range(block // part):
            lanes = slice(piece * LANES, (piece + 1) * LANES)
            out_refs[k][:part, lanes] = factor[piece * part : (piece + 1) * part, :]
        large = cols_ref[jnp.maximum((me_ref[1] ^ k) - half, 0)]
        out_refs[k][part : part + block, :] = large[:, :cols]
        out_refs[k][part + block :, :] = large[:, cols:]


def space_sum_body(n, *refs):
    ins, outs, (out_ref, weight_ref) = refs[:n], list(refs[n:-2]), refs[-2:]
    outs = [ref.at[0] if len(ref.shape) == 3 else ref for ref in outs]
    cols = ins[0].shape[1]
    width = out_ref.shape[1] - LANES - cols
    block = out_ref.shape[0] - 16
    part = ins[0].shape[0] - 2 * block
    for piece in range(2):
        at = slice(part + piece * block, part + (piece + 1) * block)
        out_ref[:block, piece * cols : (piece + 1) * cols] = sum(ref[at, :].astype(F32) for ref in ins).astype(BF16)
    for piece in range(block // part):
        lanes = slice(piece * LANES, (piece + 1) * LANES)
        factor = pack(sum(unpack(ref[:part, lanes]) for ref in ins))
        out_ref[piece * part : (piece + 1) * part, width : width + LANES] = factor
    out_ref[block:, : width + LANES] = jnp.zeros((16, width + LANES), BF16)
    total = sum(ref[...].astype(F32) for ref in outs)
    out_ref[:block, width + LANES :] = total[:block, :].astype(BF16)
    out_ref[block:, width + LANES :] = three_rows(jnp.sum(total[block : block + 16, :], axis=0, keepdims=True))
    weight_ref[...] = total[block + 16 :, :]


def add_body(n, keep_ref, got_ref, *refs):
    for j, out_ref in enumerate(refs):
        out_ref[...] = (keep_ref[j + 1].astype(F32) + got_ref[j + 1].astype(F32)).astype(BF16)


def final_body(n_var, n_space, scale, me_ref, even_ref, odd_ref, query_ref, wk_ref, kv_ref, gq_ref, out_ref, gain_ref):
    me_v, me_s = me_ref[0], me_ref[1]
    half = n_space // 2
    width = wk_ref.shape[1]
    size = width // HEADS
    cols, qcols = kv_ref.shape[1], gq_ref.shape[1]
    place = pl.multiple_of(jnp.minimum(me_s, half - 1) * cols, LANES)
    spread_kv = spread_matrix(cols, size, place)
    qplace = pl.multiple_of(me_s * qcols, LANES)
    spread_q = spread_matrix(qcols, size, qplace)
    query = query_ref[:, pl.ds(place, cols)] * scale
    block = even_ref.shape[1] - 16
    total, gain = 0.0, 0.0
    for k in range(n_var):
        part_ref, slot = (odd_ref if k % 2 else even_ref), k // 2
        at = pl.ds(pl.multiple_of((me_v ^ k) * block, block), block)
        packed = part_ref[slot, :block, cols : cols + LANES]
        key_grad = mm(packed, spread_kv) * query
        kv_ref[at, :] = jnp.where(me_s < half, key_grad, part_ref[slot, :block, :cols].astype(F32))
        keys = wk_ref[at, pl.ds(qplace, qcols)].astype(F32)
        total = total + jnp.sum(mm(packed, spread_q) * keys, axis=0, keepdims=True)
        out_ref[at, :] = part_ref[slot, :block, cols + LANES :].astype(F32)
        gain = gain + jnp.sum(part_ref[slot, block:, cols + LANES :].astype(F32), axis=0, keepdims=True)
    gq_ref[...] = total * scale
    gain_ref[...] = gain


def shards(
    patches, embed_weight, var_embed, agg_query, agg_kv, agg_out, norm_gain, qkv_weight, out_weight, cotangent
):
    n_var, n_space = lax.axis_size("var"), lax.axis_size("space")
    count, rows, pixels = patches.shape
    width = agg_out.shape[0]
    size = width // HEADS
    scale = 1.0 / math.sqrt(size)
    block = rows // n_var
    cols = width // n_space
    group = out_weight.shape[0]
    drows = width // n_var
    positions = rows * n_space
    kv_cols = 2 * width // n_space
    me = jnp.stack([lax.axis_index("var"), lax.axis_index("space")]).astype(jnp.int32)
    gain = norm_gain.reshape(1, width)
    query = agg_query.reshape(1, width)
    vmem = pl.BlockSpec(memory_space=pltpu.VMEM)
    packet = width + LANES

    whole = lambda shape: pl.BlockSpec(shape, lambda v: (0,) * len(shape))
    every = lambda shape: pl.BlockSpec((1,) + shape, lambda v: (v,) + (0,) * len(shape))
    n_chip = n_var // 2
    half = count // 2

    dattn, cot_own, w_heads = call(
        early_body,
        [struct((rows, group), BF16), struct((block, width), BF16), struct(qkv_weight.shape, BF16)],
        limit=LIMITS["early"],
        grid=(1,),
        in_specs=[SMEM] + [whole(x.shape) for x in (cotangent, out_weight, qkv_weight)],
        out_specs=[whole((rows, group)), whole((block, width)), whole(qkv_weight.shape)],
        cost_estimate=cost(2e8, 4e6),
        name="early",
    )(me, cotangent, out_weight, qkv_weight)
    dattn_all = gather_direct(dattn, "space")

    def forward_outs(here):
        return [struct((here, rows, width), BF16), struct((here, rows, width), F32), struct((here, rows, LANES), F32)]

    tokens0, value0, scores0, w_query, w_back, *state0 = call(
        functools.partial(first_body, scale),
        forward_outs(half)
        + [struct((width, 3 * LANES), BF16), struct((width, LANES), BF16)]
        + [struct((rows, width), F32), struct((rows, LANES), F32), struct((rows, LANES), F32)],
        limit=LIMITS["forward"],
        cost_estimate=cost(6e9, 2e7),
        name="forward_first",
    )(patches, embed_weight, var_embed, query, agg_kv)
    tokens1, value1, scores1, keep, send = call(
        functools.partial(second_body, half),
        forward_outs(count - half) + [struct((n_chip, block, packet), F32)] * 2,
        limit=LIMITS["forward"],
        after=dattn_all[1:],
        in_specs=[SMEM] + [vmem] * 8,
        scratch_shapes=[pltpu.VMEM((rows, width), F32), pltpu.VMEM((rows, LANES), F32)],
        cost_estimate=cost(4e9, 1e7),
        name="forward_second",
    )(me, patches, embed_weight, var_embed, w_query, agg_kv, *state0)

    def pool_pairs(mine, got):
        return call(
            pool_pair_body,
            [struct((block, packet), F32)] * n_chip,
            limit=LIMITS["pool_pair"],
            in_specs=[SMEM, vmem, vmem],
            cost_estimate=cost(1e8, 3e6),
            name="pool_pair",
        )(me, mine, got)

    received = exchange_pairs(keep, send, pool_pairs)
    mixed, pooled_packet = call(
        functools.partial(pool_body, n_chip),
        [struct((block, width), F32), struct((block, packet), BF16)],
        limit=LIMITS["pool"],
        cost_estimate=cost(1e8, 2e6),
        name="pool",
    )(*received)
    pooled_even, pooled_odd = gather_pairs(pooled_packet, "var")

    qkv, normed, pooled_packets, centred, inv = call(
        norm_body,
        [
            struct((rows, 3 * group), BF16),
            struct((rows, width), BF16),
            struct((rows, packet), BF16),
            struct((block, width), F32),
            struct((block, LANES), F32),
        ],
        limit=LIMITS["norm"],
        in_specs=[SMEM] + [vmem] * 5,
        scratch_shapes=[pltpu.VMEM((rows, width), F32), pltpu.VMEM((rows, LANES), F32)],
        cost_estimate=cost(8e8, 5e6),
        name="norm",
    )(me, pooled_even, pooled_odd, agg_out, gain, w_heads)

    qkv_all = gather_direct(qkv, "space")
    normed_cols = call(
        functools.partial(columns_body, n_space),
        [struct((rows, cols), BF16)] * n_space,
        limit=LIMITS["columns"],
        after=qkv_all[1:],
        in_specs=[SMEM, vmem],
        scratch_shapes=[pltpu.VMEM((n_space, rows, cols), BF16)],
        cost_estimate=cost(1e6, 1e6),
        name="columns",
    )(me, normed)
    normed_all = exchange_direct(normed_cols, "space")
    attn, dqkv = call(
        functools.partial(attention_body, n_space, size, scale),
        [struct((positions, group), BF16), struct((positions, 3 * group), BF16)],
        limit=LIMITS["attention"],
        after=[normed_cols[0]],
        scratch_shapes=[pltpu.VMEM((positions, group), BF16)] * 2 + [pltpu.VMEM((positions, group), F32)] * 2,
        cost_estimate=cost(6e9, 4e6),
        name="attention",
    )(*qkv_all, *dattn_all)
    dn_keep, dn_send = call(
        dn_body,
        [struct((n_chip, block, width), BF16)] * 2,
        limit=LIMITS["dn"],
        after=normed_all[1:],
        grid=(1,),
        in_specs=[SMEM, pl.BlockSpec((rows, 3 * group), lambda i: (0, 0)), vmem],
        scratch_shapes=[pltpu.VMEM((rows, width), BF16)],
        cost_estimate=cost(2e8, 1e6),
        name="dn",
    )(me, dqkv, w_heads)

    def dn_pairs(mine, got):
        return call(
            dn_pair_body,
            [struct((block, width), BF16)] * n_chip,
            limit=LIMITS["dn_pair"],
            in_specs=[SMEM, vmem, vmem],
            cost_estimate=cost(1e6, 1e6),
            name="dn_pair",
        )(me, mine, got)

    dn_received = exchange_pairs(dn_keep, dn_send, dn_pairs)
    joined_packet, dgain = call(
        functools.partial(joined_body, n_chip),
        [struct((block, packet), BF16), struct((8, width), F32)],
        limit=LIMITS["joined"],
        cost_estimate=cost(2e8, 3e6),
        name="joined",
    )(*dn_received, centred, inv, gain, cot_own, mixed, agg_out)
    joined_even, joined_odd = gather_pairs(joined_packet, "var")

    d_joined, d_pooled, stat = call(
        prepare_body,
        [struct((rows, packet), BF16), struct((rows, width), F32), struct((3, rows, LANES), F32)],
        limit=LIMITS["prepare"],
        in_specs=[SMEM] + [vmem] * 4,
        cost_estimate=cost(6e8, 4e6),
        name="prepare",
    )(me, pooled_packets, joined_even, joined_odd, agg_out)
    height = drows + 16 + group
    out_keep, out_send = call(
        out_grad_body,
        [struct((n_space // 2, height, cols), BF16)] * 2,
        limit=LIMITS["out_grad"],
        grid=(1,),
        in_specs=[SMEM] + [whole(x.shape) for x in (pooled_packets, d_joined, dgain)] + [whole((rows, group)), whole((rows, width))],
        out_specs=[whole((n_space // 2, height, cols))] * 2,
        scratch_shapes=[pltpu.VMEM((width, width), F32), pltpu.VMEM((n_space, height, cols), BF16)],
        cost_estimate=cost(6e8, 3e6),
        name="out_grad",
    )(me, pooled_packets, d_joined, dgain, attn, cotangent)
    out_got = swap(out_send, "space", 1)

    def out_add(mine, got):
        return call(
            functools.partial(out_add_body, drows),
            [struct((height, cols), BF16)] * (mine.shape[0] - 1),
            cost_estimate=cost(1e6, 1e6),
            name="out_add",
        )(mine, got)

    later, bit = out_add(out_keep, out_got), 2
    out_later, out_parts = later, [out_keep, out_got]
    while bit < n_space:
        got = {j: swap(later[j], "space", bit) for j in range(0, len(later), 2)}
        out_parts.append(got[0])
        rest = list(range(1, len(later), 2))
        if rest:
            mine = jnp.stack([later[0]] + [later[j] for j in rest])
            later = out_add(mine, jnp.stack([later[0]] + [got[j + 1] for j in rest]))
        bit *= 2

    def d_values(value, scores, after):
        here = value.shape[0]
        return call(
            dvalue_body,
            [struct((here, rows, width), BF16), struct((here, rows, 2 * LANES), BF16)],
            limit=LIMITS["dvalue"],
            after=after,
            grid=(here,),
            in_specs=[whole((rows, width)), whole((3, rows, LANES)), every((rows, width)), every((rows, LANES))],
            out_specs=[every((rows, width)), every((rows, 2 * LANES))],
            scratch_shapes=[pltpu.VMEM((LANES, width), BF16), pltpu.VMEM((width, LANES), BF16)],
            cost_estimate=cost(2e9, 5e6),
            name="dvalue",
        )(d_pooled, stat, value, scores)

    def embed(start, d_value, d_logit, after):
        here = d_value.shape[0]
        at = lambda shape: pl.BlockSpec((1,) + shape, lambda v: (v + start,) + (0,) * len(shape))
        blocks = (n_space // 2, here * pixels + 16, cols)
        return call(
            functools.partial(embed_body, n_space),
            [struct(blocks, BF16)] * 2,
            limit=LIMITS["embed"],
            after=after,
            grid=(here,),
            in_specs=[
                SMEM,
                every((rows, width)),
                every((rows, 2 * LANES)),
                at((rows, pixels)),
                pl.BlockSpec((width, width), lambda v: (0, 1)),
                whole((width, LANES)),
            ],
            out_specs=[whole(blocks)] * 2,
            scratch_shapes=[pltpu.VMEM((n_space, pixels, cols), BF16), pltpu.VMEM((16, width), F32)],
            cost_estimate=cost(1.5e9, 4e6),
            name="embed",
        )(me, d_value, d_logit, patches, agg_kv, w_back)

    dv0, dl0 = d_values(value0, scores0, [out_keep])
    dv1, dl1 = d_values(value1, scores1, [])

    step = max(drows, 256)
    kv_keep, kv_send = call(
        value_grad_body,
        [struct((n_chip, drows, packet), BF16)] * 2,
        limit=LIMITS["value_grad"],
        after=out_later,
        grid=(width // step,),
        in_specs=[SMEM]
        + [pl.BlockSpec(x.shape[:2] + (step,), lambda i: (0, 0, i)) for x in (tokens0, tokens1)]
        + [whole(x.shape) for x in (dv0, dv1, dl0, dl1)],
        out_specs=[whole((n_chip, drows, packet))] * 2,
        scratch_shapes=[pltpu.VMEM((step, packet), BF16)],
        cost_estimate=cost(4e9, 1e7),
        name="value_grad",
    )(me, tokens0, tokens1, dv0, dv1, dl0, dl1)
    kv_got = swap(kv_send, "var", 1)

    def scatter_embed(keep, arrived, after):
        n = n_space // 2 - 1
        sums = call(
            functools.partial(add_body, n),
            [struct(keep.shape[1:], BF16)] * n,
            limit=LIMITS["add"],
            after=after,
            cost_estimate=cost(1e6, 1e6),
            name="add",
        )(keep, arrived)
        blocks = {2 * (j + 1): sums[j] for j in range(n)}
        mine, bit = [keep, arrived], 2
        while bit < n_space:
            got = {k ^ bit: swap(blocks[k], "space", bit) for k in blocks if k & bit and k % bit == 0}
            mine.append(got[0])
            for k in got:
                if k:
                    blocks[k] = (blocks[k].astype(F32) + got[k].astype(F32)).astype(BF16)
            bit *= 2
        return mine, list(sums)

    keep0, send0 = embed(0, dv0, dl0, [kv_keep])
    arrived0 = swap(send0, "space", 1)
    kv_blocks = call(
        functools.partial(pair_sum_body, n_chip),
        [struct((drows, packet), BF16)] * n_chip,
        limit=LIMITS["pair_sum"],
        after=[keep0],
        in_specs=[SMEM] + [vmem] * 2,
        cost_estimate=cost(1e6, 1e6),
        name="pair_sum",
    )(me, kv_keep, kv_got)
    kv_parts = [kv_blocks[0]] + [swap(kv_blocks[k], "var", 2 * k) for k in range(1, n_chip)]
    keep1, send1 = embed(half, dv1, dl1, [kv_blocks[0]] + out_parts[2:])
    arrived1 = swap(send1, "space", 1)
    part = drows * LANES // cols
    pieces = call(
        functools.partial(packet_split_body, n_chip, n_space),
        [struct((part + 2 * drows, cols), BF16)] * n_space,
        limit=LIMITS["packet_split"],
        in_specs=[SMEM] + [vmem] * n_chip,
        scratch_shapes=[pltpu.VMEM((n_space // 2, drows, kv_cols), BF16)],
        cost_estimate=cost(1e6, 1e6),
        name="packet_split",
    )(me, *kv_parts)
    pieces_all = exchange_direct(pieces, "space")
    mine0, sums0 = scatter_embed(keep0, arrived0, [pieces[0]])
    mine1, sums1 = scatter_embed(keep1, arrived1, sums0)
    grad_qkv, head_flag = call(
        functools.partial(head_grads_body, n_space),
        [struct((cols, 3 * group), F32), struct((8, LANES), F32)],
        limit=LIMITS["head_grads"],
        cost_estimate=cost(1e9, 3e6),
        name="head_grads",
    )(*normed_all, dqkv)
    first_slot = lambda x: pl.BlockSpec((1,) + x.shape[1:], lambda i: (0, 0, 0)) if x.ndim == 3 else whole(x.shape)
    kv_sum, grad_out = call(
        functools.partial(space_sum_body, n_space),
        [struct((drows + 16, kv_cols + LANES + cols), BF16), struct((group, cols), F32)],
        limit=LIMITS["space_sum"],
        after=sums1 + [head_flag],
        grid=(1,),
        in_specs=[first_slot(x) for x in list(pieces_all) + out_parts],
        cost_estimate=cost(1e6, 1e6),
        name="space_sum",
    )(*pieces_all, *out_parts)

    def stack(parts):
        return call(
            stack_body,
            struct((len(parts),) + parts[0].shape, BF16),
            after=mine0[2:] + mine1[2:],
            cost_estimate=cost(1e6, 1e6),
            name="stack",
        )(*parts)

    kv_even, kv_odd = gather_pairs(kv_sum, "var", stack)
    grad_agg_kv, grad_query, grad_agg_out, grad_gain = call(
        functools.partial(final_body, n_var, n_space, scale),
        [struct((width, kv_cols), F32), struct((1, cols), F32)] + [struct((width, cols), F32), struct((1, cols), F32)],
        grid=(1,),
        in_specs=[SMEM] + [vmem] * 3 + [pl.BlockSpec((width, width), lambda i: (0, 0))],
        limit=LIMITS["final"],
        cost_estimate=cost(2e8, 5e6),
        name="final",
    )(me, kv_even, kv_odd, query, agg_kv)

    def first_block(x):
        if x.ndim == 3:
            return pl.BlockSpec((1,) + x.shape[1:], lambda i: (0, 0, 0))
        return pl.BlockSpec(x.shape, lambda i: (0, 0))

    grad_embed, grad_var_embed = call(
        functools.partial(embed_final_body, len(mine0)),
        [struct((count, pixels, cols), F32), struct((count, cols), F32)],
        grid=(1,),
        in_specs=[first_block(x) for x in mine0 + mine1],
        limit=LIMITS["embed_final"],
        cost_estimate=cost(1e6, 1e6),
        name="embed_final",
    )(*mine0, *mine1)

    return (
        grad_embed,
        grad_var_embed,
        grad_query.reshape(cols),
        grad_agg_kv,
        grad_agg_out,
        grad_gain.reshape(cols),
        grad_qkv,
        grad_out,
    )


def solution(mesh):
    return jax.shard_map(
        shards,
        mesh=mesh,
        in_specs=(
            P("var", "space", None),
            P("var", None, None),
            P("var", None),
            P(),
            P(),
            P(),
            P(),
            P(None, "var"),
            P("var", None),
            P("space", None),
        ),
        out_specs=(
            P("var", None, "space"),
            P("var", "space"),
            P("space"),
            P(None, "space"),
            P(None, "space"),
            P("space"),
            P("space", "var"),
            P("var", "space"),
        ),
        check_vma=False,
    )
```

profile of v0, /device:TPU:0, one launch (start us, length us, event | category | flops | bytes accessed | tf_op | source)
XLA Modules:
  0.0 223.4 jit_solution(11437521090086788837)
XLA Ops:
  1.3 3.0 %early.1 = (bf16[256,128]{1,0:T(8,128)(2,1)}, bf16[32,1024]{1,0:T(8,128)(2,1)}, bf16[1024,384]{1,0:T(8,128)(2,1)}) custom-call(s32[2]{0:T(128)} %pad_add_fusion.refs_0_, bf16[256,1024]{1,0:T(8,128)(2,1)} %refs_5_.3, bf16[128,1024]{1,0:T(8,128)(2,1)} %refs_2_.4, bf16[1024,384]{1,0:T(8,128)(2,1)} %refs_3_.5), custom_call_target="tpu_custom_call" | custom-call | flops 200000000 | bytes 4000000 | tf_op jit(solution)/shard_map/early/pallas_call | solution.py:84
  4.3 3.0 %collective-permute-start = (bf16[256,128]{1,0:T(8,128)(2,1)}, bf16[256,128]{1,0:T(8,128)(2,1)S(1)}, u32[]{:S(2)}, u32[]{:S(2)}) collective-permute-start(bf16[256,128]{1,0:T(8,128)(2,1)} %get-tuple-element.86.refs_4_), channel_id=1, source_target_pairs={{0,1},{1,0},{2,3},{3,2},{4,5},{5,4},{6,7},{7,6},{8,9},{9,8},{10,11... | collective-permute-start | bytes 196616 | tf_op jit(solution)/shard_map/ppermute | solution.py:110
  7.3 2.6 %collective-permute-start.1 = (bf16[256,128]{1,0:T(8,128)(2,1)}, bf16[256,128]{1,0:T(8,128)(2,1)S(1)}, u32[]{:S(2)}, u32[]{:S(2)}) collective-permute-start(bf16[256,128]{1,0:T(8,128)(2,1)} %get-tuple-element.86.refs_4_), channel_id=1, source_target_pairs={{0,2},{1,3},{2,0},{3,1},{4,6},{5,7},{6,4},{7,5},{8,10},{9,11},{10,... | collective-permute-start | bytes 196616 | tf_op jit(solution)/shard_map/ppermute | solution.py:110
  9.9 2.2 copy-done
  12.1 1.9 copy-done.10
  14.0 8.1 %forward_first.1 = (bf16[3,256,1024]{2,1,0:T(8,128)(2,1)S(1)}, f32[3,256,1024]{2,1,0:T(8,128)S(1)}, f32[3,256,128]{2,1,0:T(8,128)S(1)}, bf16[1024,384]{1,0:T(8,1...) custom-call(bf16[6,256,256]{2,1,0:T(8,128)(2,1)S(1)} %copy-done.3, ...), custom_call_target="tpu_custom_call" | custom-call | flops 6000000000 | bytes 20000000 | tf_op jit(solution)/shard_map/forward_first/pallas_call | solution.py:84
  22.2 4.7 %forward_second.1 = (bf16[3,256,1024]{2,1,0:T(8,128)(2,1)S(1)}, f32[3,256,1024]{2,1,0:T(8,128)S(1)}, f32[3,256,128]{2,1,0:T(8,128)S(1)}, f32[4,32,1152]{2,1,0:T(8,128)S(1)}, f32[4,32,1152]{2,1,0:T(8,128)S(1)}) custom-call(s32[2]{0:T(128)S(1)} %copy-done.6, bf16[6,256,256]{2,1,0:T(8,128)(2,1)S(1)} %copy-done.3, bf16[6,256,1024]{2,1,0:T(8,128)(2,1)S(1)} %copy-done.10, ...), custom_call_target="tpu_custom_call" | custom-call | flops 4000000000 | bytes 10000000 | tf_op jit(solution)/shard_map/forward_second/pallas_call | solution.py:84
  27.0 2.0 collective-permute-done.3.refs_2_
  33.4 2.9 %collective-permute-done.4.refs_1_ = f32[32,1152]{1,0:T(8,128)S(1)} collective-permute-done((f32[32,1152]{1,0:T(8,128)S(1)}, f32[32,1152]{1,0:T(8,128)S(1)}, u32[]{:S(2)}, u32[]{:S(2)}) %collective-permute-start.4) | collective-permute-done | bytes 147488 | tf_op jit(solution)/shard_map/ppermute | solution.py:110
  36.3 4.1 %collective-permute-done.5.refs_2_ = f32[32,1152]{1,0:T(8,128)S(1)} collective-permute-done((f32[32,1152]{1,0:T(8,128)S(1)}, f32[32,1152]{1,0:T(8,128)S(1)}, u32[]{:S(2)}, u32[]{:S(2)}) %collective-permute-start.5) | collective-permute-done | bytes 147488 | tf_op jit(solution)/shard_map/ppermute | solution.py:110
  49.8 10.6 %norm.1 = (bf16[256,384]{1,0:T(8,128)(2,1)S(1)}, bf16[256,1024]{1,0:T(8,128)(2,1)S(1)}, bf16[256,1152]{1,0:T(8,128)(2,1)S(1)}, f32[32,1024]{1,0:T(8,128)S(1)}, f32[32,128]{1,0:T(8,128)S(1)}) custom-call(s32[2]{0:T(128)S(1)} %copy-done.6, bf16[4,32,1152]{2,1,0:T(8,128)(2,1)S(1)} %pad_maximum_fusion.refs_1_, ...), custom_call_target="tpu_custom_call" | custom-call | flops 800000000 | bytes 5000000 | tf_op jit(solution)/shard_map/norm/pallas_call | solution.py:84
  61.2 3.5 %collective-permute-start.12 = (bf16[256,384]{1,0:T(8,128)(2,1)S(1)}, bf16[256,384]{1,0:T(8,128)(2,1)S(1)}, u32[]{:S(2)}, u32[]{:S(2)}) collective-permute-start(bf16[256,384]{1,0:T(8,128)(2,1)S(1)} %get-tuple-element.96.refs_0_), channel_id=1, source_target_pairs={{0,2},{1,3},{2,0},{3,1},{4,6},{5,7},{6,4},{7,5},{8,10},{9,11},{10,... | collective-permute-start | bytes 589832 | tf_op jit(solution)/shard_map/ppermute | solution.py:110
  64.9 6.2 %collective-permute-done.11.refs_2_.refs_1_ = bf16[256,384]{1,0:T(8,128)(2,1)S(1)} collective-permute-done((bf16[256,384]{1,0:T(8,128)(2,1)S(1)}, bf16[256,384]{1,0:T(8,128)(2,1)S(1)}, u32[]{:S(2)}, u32[]{:S(2)}) %collective-permute-start.11) | collective-permute-done | bytes 196640 | tf_op jit(solution)/shard_map/ppermute | solution.py:110
  71.2 7.7 %collective-permute-done.12.refs_3_.refs_2_ = bf16[256,384]{1,0:T(8,128)(2,1)S(1)} collective-permute-done((bf16[256,384]{1,0:T(8,128)(2,1)S(1)}, bf16[256,384]{1,0:T(8,128)(2,1)S(1)}, u32[]{:S(2)}, u32[]{:S(2)}) %collective-permute-start.12) | collective-permute-done | bytes 196640 | tf_op jit(solution)/shard_map/ppermute | solution.py:110
  79.5 4.0 %collective-permute-start.14 = (bf16[256,256]{1,0:T(8,128)(2,1)S(1)}, bf16[256,256]{1,0:T(8,128)(2,1)S(1)}, u32[]{:S(2)}, u32[]{:S(2)}) collective-permute-start(bf16[256,256]{1,0:T(8,128)(2,1)S(1)} %get-tuple-element.100), channel_id=1, source_target_pairs={{0,1},{1,0},{2,3},{3,2},{4,5},{5,4},{6,7},{7,6},{8,9},{9,8},{10,11... | collective-permute-start | bytes 393224 | tf_op jit(solution)/shard_map/ppermute | solution.py:110
  86.0 10.9 %attention.1 = (bf16[1024,128]{1,0:T(8,128)(2,1)S(1)}, bf16[1024,384]{1,0:T(8,128)(2,1)S(1)}) custom-call(bf16[256,384]{1,0:T(8,128)(2,1)S(1)} %get-tuple-element.96.refs_0_, bf16[256,384]{1,0:T(8,128)(2,1)S(1)} %collective-permute-done.11.refs_2_.refs_1_, bf16[256,384]{1,0:T(8,128)(2,1)S(1)} %collective-permute-done.12.refs_3_.refs_2_, ...), custom_call_target="tpu_custom_call" | custom-call | flops 6000000000 | bytes 4000000 | tf_op jit(solution)/shard_map/attention/pallas_call | solution.py:84
  104.5 2.2 collective-permute-done.19.refs_2_
  113.4 2.0 collective-permute-done.23
  121.3 2.6 %dvalue.3 = (bf16[3,256,1024]{2,1,0:T(8,128)(2,1)S(1)}, bf16[3,256,256]{2,1,0:T(8,128)(2,1)S(1)}) custom-call(f32[256,1024]{1,0:T(8,128)S(1)} %get-tuple-element.114.refs_0_, f32[3,256,128]{2,1,0:T(8,128)S(1)} %get-tuple-element.115.refs_1_, f32[3,256,1024]{2,1,0:T(8,128)S(1)} %get-tuple-element.127.refs_2_, f32[3,256,128]{2,1,0:T(8,128)S(1)} %get-tuple-element.128.refs_3_), custom_call_target="tpu_custom_call" | custom-call | flops 2000000000 | bytes 5000000 | tf_op jit(solution)/shard_map/dvalue/pallas_call | solution.py:84
  123.9 2.6 %dvalue.2 = (bf16[3,256,1024]{2,1,0:T(8,128)(2,1)S(1)}, bf16[3,256,256]{2,1,0:T(8,128)(2,1)S(1)}) custom-call(f32[256,1024]{1,0:T(8,128)S(1)} %get-tuple-element.114.refs_0_, f32[3,256,128]{2,1,0:T(8,128)S(1)} %get-tuple-element.115.refs_1_, f32[3,256,1024]{2,1,0:T(8,128)S(1)} %get-tuple-element.116.refs_2_, f32[3,256,128]{2,1,0:T(8,128)S(1)} %get-tuple-element.117.refs_3_, ...), custom_call_target="tpu_custom_call" | custom-call | flops 2000000000 | bytes 5000000 | tf_op jit(solution)/shard_map/dvalue/pallas_call | solution.py:84
  126.5 2.4 %collective-permute-done.25.refs_1_.refs_5_ = bf16[2,272,256]{2,1,0:T(8,128)(2,1)S(1)} collective-permute-done((bf16[2,272,256]{2,1,0:T(8,128)(2,1)S(1)}, bf16[2,272,256]{2,1,0:T(8,128)(2,1)S(1)}, u32[]{:S(2)}, u32[]{:S(2)}) %collective-permute-start.25) | collective-permute-done | bytes 278560 | tf_op jit(solution)/shard_map/ppermute | solution.py:110
  129.0 6.1 %value_grad.1 = (bf16[4,128,1152]{2,1,0:T(8,128)(2,1)S(1)}, bf16[4,128,1152]{2,1,0:T(8,128)(2,1)S(1)}) custom-call(s32[2]{0:T(128)S(1)} %copy-done.6, bf16[3,256,1024]{2,1,0:T(8,128)(2,1)S(1)} %get-tuple-element.125.refs_1_, bf16[3,256,1024]{2,1,0:T(8,128)(2,1)S(1)} %get-tuple-element.126.refs_2_, ...), custom_call_target="tpu_custom_call" | custom-call | flops 4000000000 | bytes 10000000 | tf_op jit(solution)/shard_map/value_grad/pallas_call | solution.py:84
  135.1 2.1 collective-permute-start.32
  137.2 4.1 %embed.2 = (bf16[2,784,256]{2,1,0:T(8,128)(2,1)S(1)}, bf16[2,784,256]{2,1,0:T(8,128)(2,1)S(1)}) custom-call(s32[2]{0:T(128)S(1)} %copy-done.6, bf16[3,256,1024]{2,1,0:T(8,128)(2,1)S(1)} %get-tuple-element.122.refs_3_.refs_1_, bf16[3,256,256]{2,1,0:T(8,128)(2,1)S(1)} %get-tuple-element.123.refs_5_.refs_2_, bf16[6,256,256]{2,1,0:T(8,128)(2,1)S(1)} %copy-done.3, ...), custom_call_target="tpu_custom_call" | custom-call | flops 1500000000 | bytes 4000000 | tf_op jit(solution)/shard_map/embed/pallas_call | solution.py:84
  145.2 4.1 %embed.3 = (bf16[2,784,256]{2,1,0:T(8,128)(2,1)S(1)}, bf16[2,784,256]{2,1,0:T(8,128)(2,1)S(1)}) custom-call(s32[2]{0:T(128)S(1)} %copy-done.6, bf16[3,256,1024]{2,1,0:T(8,128)(2,1)S(1)} %get-tuple-element.129.refs_4_.refs_1_, bf16[3,256,256]{2,1,0:T(8,128)(2,1)S(1)} %get-tuple-element.130.refs_6_.refs_2_, bf16[6,256,256]{2,1,0:T(8,128)(2,1)S(1)} %copy-done.3, ...), custom_call_target="tpu_custom_call" | custom-call | flops 1500000000 | bytes 4000000 | tf_op jit(solution)/shard_map/embed/pallas_call | solution.py:84
  152.9 6.4 %collective-permute-done.28.refs_2_ = bf16[128,1152]{1,0:T(8,128)(2,1)S(1)} collective-permute-done((bf16[128,1152]{1,0:T(8,128)(2,1)S(1)}, bf16[128,1152]{1,0:T(8,128)(2,1)S(1)}, u32[]{:S(2)}, u32[]{:S(2)}) %collective-permute-start.28) | collective-permute-done | bytes 294944 | tf_op jit(solution)/shard_map/ppermute | solution.py:110
  159.3 4.5 %collective-permute-done.29.refs_3_ = bf16[128,1152]{1,0:T(8,128)(2,1)S(1)} collective-permute-done((bf16[128,1152]{1,0:T(8,128)(2,1)S(1)}, bf16[128,1152]{1,0:T(8,128)(2,1)S(1)}, u32[]{:S(2)}, u32[]{:S(2)}) %collective-permute-start.29) | collective-permute-done | bytes 294944 | tf_op jit(solution)/shard_map/ppermute | solution.py:110
  172.0 21.1 %collective-permute-done.33.refs_1_.refs_4_ = bf16[2,784,256]{2,1,0:T(8,128)(2,1)S(1)} collective-permute-done((bf16[2,784,256]{2,1,0:T(8,128)(2,1)S(1)}, bf16[2,784,256]{2,1,0:T(8,128)(2,1)S(1)}, u32[]{:S(2)}, u32[]{:S(2)}) %collective-permute-start.33) | collective-permute-done | bytes 802848 | tf_op jit(solution)/shard_map/ppermute | solution.py:110
  197.7 2.5 %collective-permute-start.39 = (bf16[144,896]{1,0:T(8,128)(2,1)S(1)}, bf16[144,896]{1,0:T(8,128)(2,1)S(1)}, u32[]{:S(2)}, u32[]{:S(2)}) collective-permute-start(bf16[144,896]{1,0:T(8,128)(2,1)S(1)} %get-tuple-element.149.refs_0_), channel_id=1, source_target_pairs={{0,16},{4,20},{8,24},{12,28},{16,0},{20,4},{24,8},{28,12},{1,17},{... | collective-permute-start | bytes 774152 | tf_op jit(solution)/shard_map/ppermute | solution.py:110
  200.9 10.1 %collective-permute-done.31.refs_2_.refs_4_ = bf16[784,256]{1,0:T(8,128)(2,1)S(1)} collective-permute-done((bf16[784,256]{1,0:T(8,128)(2,1)S(1)}, bf16[784,256]{1,0:T(8,128)(2,1)S(1)}, u32[]{:S(2)}, u32[]{:S(2)}) %collective-permute-start.31) | collective-permute-done | bytes 401440 | tf_op jit(solution)/shard_map/ppermute | solution.py:110
  211.9 5.6 %collective-permute-done.34.refs_5_ = bf16[784,256]{1,0:T(8,128)(2,1)S(1)} collective-permute-done((bf16[784,256]{1,0:T(8,128)(2,1)S(1)}, bf16[784,256]{1,0:T(8,128)(2,1)S(1)}, u32[]{:S(2)}, u32[]{:S(2)}) %collective-permute-start.34) | collective-permute-done | bytes 401440 | tf_op jit(solution)/shard_map/ppermute | solution.py:110
  220.3 2.8 %final.1 = (f32[1024,512]{1,0:T(8,128)}, f32[1,256]{1,0:T(1,128)}, f32[1024,256]{1,0:T(8,128)}, f32[1,256]{1,0:T(1,128)}) custom-call(s32[2]{0:T(128)S(1)} %copy-done.6, bf16[4,144,896]{2,1,0:T(8,128)(2,1)S(1)} %stack.53.refs_1_, bf16[4,144,896]{2,1,0:T(8,128)(2,1)S(1)} %collective-permute-done.41.refs_2_, f32[1,1024]{1,0:T(1,128)S(1)} %bitcast.19, ...), custom_call_target="tpu_custom_call" | custom-call | flops 200000000 | bytes 5000000 | tf_op jit(solution)/shard_map/final/pallas_call | solution.py:84
  (109 shorter events, 63.4 us)
Async XLA Ops:
  4.3 17.8 %collective-permute-start = (bf16[256,128]{1,0:T(8,128)(2,1)}, bf16[256,128]{1,0:T(8,128)(2,1)S(1)}, u32[]{:S(2)}, u32[]{:S(2)}) collective-permute-start(bf16[256,128]{1,0:T(8,128)(2,1)} %get-tuple-element.86.refs_4_), channel_id=1, source_target_pairs={{0,1},{1,0},{2,3},{3,2},{4,5},{5,4},{6,7},{7,6},{8,9},{9,8},{10,11... | collective-permute-start | bytes 196616 | tf_op jit(solution)/shard_map/ppermute | solution.py:110
  7.3 14.8 %collective-permute-start.1 = (bf16[256,128]{1,0:T(8,128)(2,1)}, bf16[256,128]{1,0:T(8,128)(2,1)S(1)}, u32[]{:S(2)}, u32[]{:S(2)}) collective-permute-start(bf16[256,128]{1,0:T(8,128)(2,1)} %get-tuple-element.86.refs_4_), channel_id=1, source_target_pairs={{0,2},{1,3},{2,0},{3,1},{4,6},{5,7},{6,4},{7,5},{8,10},{9,11},{10,... | collective-permute-start | bytes 196616 | tf_op jit(solution)/shard_map/ppermute | solution.py:110
  9.9 12.2 %collective-permute-start.2 = (bf16[256,128]{1,0:T(8,128)(2,1)}, bf16[256,128]{1,0:T(8,128)(2,1)S(1)}, u32[]{:S(2)}, u32[]{:S(2)}) collective-permute-start(bf16[256,128]{1,0:T(8,128)(2,1)} %get-tuple-element.86.refs_4_), channel_id=1, source_target_pairs={{0,3},{1,2},{2,1},{3,0},{4,7},{5,6},{6,5},{7,4},{8,11},{9,10},{10,... | collective-permute-start | bytes 196616 | tf_op jit(solution)/shard_map/ppermute | solution.py:110
  29.9 6.4 %collective-permute-start.4 = (f32[32,1152]{1,0:T(8,128)S(1)}, f32[32,1152]{1,0:T(8,128)S(1)}, u32[]{:S(2)}, u32[]{:S(2)}) collective-permute-start(f32[32,1152]{1,0:T(8,128)S(1)} %get-tuple-element.90), channel_id=1, source_target_pairs={{0,8},{4,12},{8,0},{12,4},{16,24},{20,28},{24,16},{28,20},{1,9},{5... | collective-permute-start | bytes 442376 | tf_op jit(solution)/shard_map/ppermute | solution.py:110
  31.6 8.8 %collective-permute-start.5 = (f32[32,1152]{1,0:T(8,128)S(1)}, f32[32,1152]{1,0:T(8,128)S(1)}, u32[]{:S(2)}, u32[]{:S(2)}) collective-permute-start(f32[32,1152]{1,0:T(8,128)S(1)} %get-tuple-element.91), channel_id=1, source_target_pairs={{0,16},{4,20},{8,24},{12,28},{16,0},{20,4},{24,8},{28,12},{1,17},{... | collective-permute-start | bytes 442376 | tf_op jit(solution)/shard_map/ppermute | solution.py:110
  33.2 7.3 %collective-permute-start.6 = (f32[32,1152]{1,0:T(8,128)S(1)}, f32[32,1152]{1,0:T(8,128)S(1)}, u32[]{:S(2)}, u32[]{:S(2)}) collective-permute-start(f32[32,1152]{1,0:T(8,128)S(1)} %get-tuple-element.92), channel_id=1, source_target_pairs={{0,24},{4,28},{8,16},{12,20},{16,8},{20,12},{24,0},{28,4},{1,25},{... | collective-permute-start | bytes 442376 | tf_op jit(solution)/shard_map/ppermute | solution.py:110
  42.8 5.3 %collective-permute-start.9 = (bf16[32,1152]{1,0:T(8,128)(2,1)S(1)}, bf16[32,1152]{1,0:T(8,128)(2,1)S(1)}, u32[]{:S(2)}, u32[]{:S(2)}) collective-permute-start(bf16[32,1152]{1,0:T(8,128)(2,1)S(1)} %get-tuple-element.93), channel_id=1, source_target_pairs={{0,24},{4,28},{8,16},{12,20},{16,8},{20,12},{24,0},{28,4},{1,25},{... | collective-permute-start | bytes 221192 | tf_op jit(solution)/shard_map/ppermute | solution.py:110
  60.5 10.7 %collective-permute-start.11 = (bf16[256,384]{1,0:T(8,128)(2,1)S(1)}, bf16[256,384]{1,0:T(8,128)(2,1)S(1)}, u32[]{:S(2)}, u32[]{:S(2)}) collective-permute-start(bf16[256,384]{1,0:T(8,128)(2,1)S(1)} %get-tuple-element.96.refs_0_), channel_id=1, source_target_pairs={{0,1},{1,0},{2,3},{3,2},{4,5},{5,4},{6,7},{7,6},{8,9},{9,8},{10,11... | collective-permute-start | bytes 589832 | tf_op jit(solution)/shard_map/ppermute | solution.py:110
  61.2 17.7 %collective-permute-start.12 = (bf16[256,384]{1,0:T(8,128)(2,1)S(1)}, bf16[256,384]{1,0:T(8,128)(2,1)S(1)}, u32[]{:S(2)}, u32[]{:S(2)}) collective-permute-start(bf16[256,384]{1,0:T(8,128)(2,1)S(1)} %get-tuple-element.96.refs_0_), channel_id=1, source_target_pairs={{0,2},{1,3},{2,0},{3,1},{4,6},{5,7},{6,4},{7,5},{8,10},{9,11},{10,... | collective-permute-start | bytes 589832 | tf_op jit(solution)/shard_map/ppermute | solution.py:110
  64.7 14.2 %collective-permute-start.13 = (bf16[256,384]{1,0:T(8,128)(2,1)S(1)}, bf16[256,384]{1,0:T(8,128)(2,1)S(1)}, u32[]{:S(2)}, u32[]{:S(2)}) collective-permute-start(bf16[256,384]{1,0:T(8,128)(2,1)S(1)} %get-tuple-element.96.refs_0_), channel_id=1, source_target_pairs={{0,3},{1,2},{2,1},{3,0},{4,7},{5,6},{6,5},{7,4},{8,11},{9,10},{10,... | collective-permute-start | bytes 589832 | tf_op jit(solution)/shard_map/ppermute | solution.py:110
  79.5 17.4 %collective-permute-start.14 = (bf16[256,256]{1,0:T(8,128)(2,1)S(1)}, bf16[256,256]{1,0:T(8,128)(2,1)S(1)}, u32[]{:S(2)}, u32[]{:S(2)}) collective-permute-start(bf16[256,256]{1,0:T(8,128)(2,1)S(1)} %get-tuple-element.100), channel_id=1, source_target_pairs={{0,1},{1,0},{2,3},{3,2},{4,5},{5,4},{6,7},{7,6},{8,9},{9,8},{10,11... | collective-permute-start | bytes 393224 | tf_op jit(solution)/shard_map/ppermute | solution.py:110
  83.5 13.4 %collective-permute-start.15 = (bf16[256,256]{1,0:T(8,128)(2,1)S(1)}, bf16[256,256]{1,0:T(8,128)(2,1)S(1)}, u32[]{:S(2)}, u32[]{:S(2)}) collective-permute-start(bf16[256,256]{1,0:T(8,128)(2,1)S(1)} %get-tuple-element.101), channel_id=1, source_target_pairs={{0,2},{1,3},{2,0},{3,1},{4,6},{5,7},{6,4},{7,5},{8,10},{9,11},{10,... | collective-permute-start | bytes 393224 | tf_op jit(solution)/shard_map/ppermute | solution.py:110
  84.6 12.3 %collective-permute-start.16 = (bf16[256,256]{1,0:T(8,128)(2,1)S(1)}, bf16[256,256]{1,0:T(8,128)(2,1)S(1)}, u32[]{:S(2)}, u32[]{:S(2)}) collective-permute-start(bf16[256,256]{1,0:T(8,128)(2,1)S(1)} %get-tuple-element.102), channel_id=1, source_target_pairs={{0,3},{1,2},{2,1},{3,0},{4,7},{5,6},{6,5},{7,4},{8,11},{9,10},{10,... | collective-permute-start | bytes 393224 | tf_op jit(solution)/shard_map/ppermute | solution.py:110
  101.8 5.0 %collective-permute-start.19 = (bf16[32,1024]{1,0:T(8,128)(2,1)S(1)}, bf16[32,1024]{1,0:T(8,128)(2,1)S(1)}, u32[]{:S(2)}, u32[]{:S(2)}) collective-permute-start(bf16[32,1024]{1,0:T(8,128)(2,1)S(1)} %get-tuple-element.107), channel_id=1, source_target_pairs={{0,16},{4,20},{8,24},{12,28},{16,0},{20,4},{24,8},{28,12},{1,17},{... | collective-permute-start | bytes 196616 | tf_op jit(solution)/shard_map/ppermute | solution.py:110
  102.3 5.2 %collective-permute-start.20 = (bf16[32,1024]{1,0:T(8,128)(2,1)S(1)}, bf16[32,1024]{1,0:T(8,128)(2,1)S(1)}, u32[]{:S(2)}, u32[]{:S(2)}) collective-permute-start(bf16[32,1024]{1,0:T(8,128)(2,1)S(1)} %get-tuple-element.108), channel_id=1, source_target_pairs={{0,24},{4,28},{8,16},{12,20},{16,8},{20,12},{24,0},{28,4},{1,25},{... | collective-permute-start | bytes 196616 | tf_op jit(solution)/shard_map/ppermute | solution.py:110
  110.2 5.3 %collective-permute-start.23 = (bf16[32,1152]{1,0:T(8,128)(2,1)S(1)}, bf16[32,1152]{1,0:T(8,128)(2,1)S(1)}, u32[]{:S(2)}, u32[]{:S(2)}) collective-permute-start(bf16[32,1152]{1,0:T(8,128)(2,1)S(1)} %get-tuple-element.113), channel_id=1, source_target_pairs={{0,24},{4,28},{8,16},{12,20},{16,8},{20,12},{24,0},{28,4},{1,25},{... | collective-permute-start | bytes 221192 | tf_op jit(solution)/shard_map/ppermute | solution.py:110
  120.1 8.8 %collective-permute-start.25 = (bf16[2,272,256]{2,1,0:T(8,128)(2,1)S(1)}, bf16[2,272,256]{2,1,0:T(8,128)(2,1)S(1)}, u32[]{:S(2)}, u32[]{:S(2)}) collective-permute-start(bf16[2,272,256]{2,1,0:T(8,128)(2,1)S(1)} %get-tuple-element.131), channel_id=1, source_target_pairs={{0,1},{1,0},{2,3},{3,2},{4,5},{5,4},{6,7},{7,6},{8,9},{9,8},{10,11... | collective-permute-start | bytes 835592 | tf_op jit(solution)/shard_map/ppermute | solution.py:110
  135.0 7.3 %collective-permute-start.27 = (bf16[4,128,1152]{2,1,0:T(8,128)(2,1)S(1)}, bf16[4,128,1152]{2,1,0:T(8,128)(2,1)S(1)}, u32[]{:S(2)}, u32[]{:S(2)}) collective-permute-start(bf16[4,128,1152]{2,1,0:T(8,128)(2,1)S(1)} %get-tuple-element.135), channel_id=1, source_target_pairs={{0,4},{4,0},{8,12},{12,8},{16,20},{20,16},{24,28},{28,24},{1,5},{5... | collective-permute-start | bytes 3538952 | tf_op jit(solution)/shard_map/ppermute | solution.py:110
  135.1 10.1 %collective-permute-start.32 = (bf16[272,256]{1,0:T(8,128)(2,1)S(1)}, bf16[272,256]{1,0:T(8,128)(2,1)S(1)}, u32[]{:S(2)}, u32[]{:S(2)}) collective-permute-start(bf16[272,256]{1,0:T(8,128)(2,1)S(1)} %out_add.1.refs_7_), channel_id=1, source_target_pairs={{0,2},{1,3},{2,0},{3,1},{4,6},{5,7},{6,4},{7,5},{8,10},{9,11},{10,... | collective-permute-start | bytes 417800 | tf_op jit(solution)/shard_map/ppermute | solution.py:110
  141.3 28.8 %collective-permute-start.26 = (bf16[2,784,256]{2,1,0:T(8,128)(2,1)S(1)}, bf16[2,784,256]{2,1,0:T(8,128)(2,1)S(1)}, u32[]{:S(2)}, u32[]{:S(2)}) collective-permute-start(bf16[2,784,256]{2,1,0:T(8,128)(2,1)S(1)} %get-tuple-element.134), channel_id=1, source_target_pairs={{0,1},{1,0},{2,3},{3,2},{4,5},{5,4},{6,7},{7,6},{8,9},{9,8},{10,11... | collective-permute-start | bytes 2408456 | tf_op jit(solution)/shard_map/ppermute | solution.py:110
  149.3 43.8 %collective-permute-start.33 = (bf16[2,784,256]{2,1,0:T(8,128)(2,1)S(1)}, bf16[2,784,256]{2,1,0:T(8,128)(2,1)S(1)}, u32[]{:S(2)}, u32[]{:S(2)}) collective-permute-start(bf16[2,784,256]{2,1,0:T(8,128)(2,1)S(1)} %get-tuple-element.142), channel_id=1, source_target_pairs={{0,1},{1,0},{2,3},{3,2},{4,5},{5,4},{6,7},{7,6},{8,9},{9,8},{10,11... | collective-permute-start | bytes 2408456 | tf_op jit(solution)/shard_map/ppermute | solution.py:110
  149.3 10.0 %collective-permute-start.28 = (bf16[128,1152]{1,0:T(8,128)(2,1)S(1)}, bf16[128,1152]{1,0:T(8,128)(2,1)S(1)}, u32[]{:S(2)}, u32[]{:S(2)}) collective-permute-start(bf16[128,1152]{1,0:T(8,128)(2,1)S(1)} %get-tuple-element.137), channel_id=1, source_target_pairs={{0,8},{4,12},{8,0},{12,4},{16,24},{20,28},{24,16},{28,20},{1,9},{5... | collective-permute-start | bytes 884744 | tf_op jit(solution)/shard_map/ppermute | solution.py:110
  150.2 13.6 %collective-permute-start.29 = (bf16[128,1152]{1,0:T(8,128)(2,1)S(1)}, bf16[128,1152]{1,0:T(8,128)(2,1)S(1)}, u32[]{:S(2)}, u32[]{:S(2)}) collective-permute-start(bf16[128,1152]{1,0:T(8,128)(2,1)S(1)} %get-tuple-element.138), channel_id=1, source_target_pairs={{0,16},{4,20},{8,24},{12,28},{16,0},{20,4},{24,8},{28,12},{1,17},{... | collective-permute-start | bytes 884744 | tf_op jit(solution)/shard_map/ppermute | solution.py:110
  151.7 13.0 %collective-permute-start.30 = (bf16[128,1152]{1,0:T(8,128)(2,1)S(1)}, bf16[128,1152]{1,0:T(8,128)(2,1)S(1)}, u32[]{:S(2)}, u32[]{:S(2)}) collective-permute-start(bf16[128,1152]{1,0:T(8,128)(2,1)S(1)} %get-tuple-element.139), channel_id=1, source_target_pairs={{0,24},{4,28},{8,16},{12,20},{16,8},{20,12},{24,0},{28,4},{1,25},{... | collective-permute-start | bytes 884744 | tf_op jit(solution)/shard_map/ppermute | solution.py:110
  165.6 30.9 %collective-permute-start.35 = (bf16[320,256]{1,0:T(8,128)(2,1)S(1)}, bf16[320,256]{1,0:T(8,128)(2,1)S(1)}, u32[]{:S(2)}, u32[]{:S(2)}) collective-permute-start(bf16[320,256]{1,0:T(8,128)(2,1)S(1)} %get-tuple-element.145), channel_id=1, source_target_pairs={{0,1},{1,0},{2,3},{3,2},{4,5},{5,4},{6,7},{7,6},{8,9},{9,8},{10,11... | collective-permute-start | bytes 491528 | tf_op jit(solution)/shard_map/ppermute | solution.py:110
  167.3 29.2 %collective-permute-start.36 = (bf16[320,256]{1,0:T(8,128)(2,1)S(1)}, bf16[320,256]{1,0:T(8,128)(2,1)S(1)}, u32[]{:S(2)}, u32[]{:S(2)}) collective-permute-start(bf16[320,256]{1,0:T(8,128)(2,1)S(1)} %get-tuple-element.146), channel_id=1, source_target_pairs={{0,2},{1,3},{2,0},{3,1},{4,6},{5,7},{6,4},{7,5},{8,10},{9,11},{10,... | collective-permute-start | bytes 491528 | tf_op jit(solution)/shard_map/ppermute | solution.py:110
  168.7 27.8 %collective-permute-start.37 = (bf16[320,256]{1,0:T(8,128)(2,1)S(1)}, bf16[320,256]{1,0:T(8,128)(2,1)S(1)}, u32[]{:S(2)}, u32[]{:S(2)}) collective-permute-start(bf16[320,256]{1,0:T(8,128)(2,1)S(1)} %get-tuple-element.147), channel_id=1, source_target_pairs={{0,3},{1,2},{2,1},{3,0},{4,7},{5,6},{6,5},{7,4},{8,11},{9,10},{10,... | collective-permute-start | bytes 491528 | tf_op jit(solution)/shard_map/ppermute | solution.py:110
  170.1 40.8 %collective-permute-start.31 = (bf16[784,256]{1,0:T(8,128)(2,1)S(1)}, bf16[784,256]{1,0:T(8,128)(2,1)S(1)}, u32[]{:S(2)}, u32[]{:S(2)}) collective-permute-start(bf16[784,256]{1,0:T(8,128)(2,1)S(1)} %add.4.refs_2_), channel_id=1, source_target_pairs={{0,2},{1,3},{2,0},{3,1},{4,6},{5,7},{6,4},{7,5},{8,10},{9,11},{10,... | collective-permute-start | bytes 1204232 | tf_op jit(solution)/shard_map/ppermute | solution.py:110
  193.1 24.3 %collective-permute-start.34 = (bf16[784,256]{1,0:T(8,128)(2,1)S(1)}, bf16[784,256]{1,0:T(8,128)(2,1)S(1)}, u32[]{:S(2)}, u32[]{:S(2)}) collective-permute-start(bf16[784,256]{1,0:T(8,128)(2,1)S(1)} %add.5.refs_7_), channel_id=1, source_target_pairs={{0,2},{1,3},{2,0},{3,1},{4,6},{5,7},{6,4},{7,5},{8,10},{9,11},{10,... | collective-permute-start | bytes 1204232 | tf_op jit(solution)/shard_map/ppermute | solution.py:110
  197.4 13.6 %collective-permute-start.38 = (bf16[144,896]{1,0:T(8,128)(2,1)S(1)}, bf16[144,896]{1,0:T(8,128)(2,1)S(1)}, u32[]{:S(2)}, u32[]{:S(2)}) collective-permute-start(bf16[144,896]{1,0:T(8,128)(2,1)S(1)} %get-tuple-element.149.refs_0_), channel_id=1, source_target_pairs={{0,8},{4,12},{8,0},{12,4},{16,24},{20,28},{24,16},{28,20},{1,9},{5... | collective-permute-start | bytes 774152 | tf_op jit(solution)/shard_map/ppermute | solution.py:110
  197.7 14.2 %collective-permute-start.39 = (bf16[144,896]{1,0:T(8,128)(2,1)S(1)}, bf16[144,896]{1,0:T(8,128)(2,1)S(1)}, u32[]{:S(2)}, u32[]{:S(2)}) collective-permute-start(bf16[144,896]{1,0:T(8,128)(2,1)S(1)} %get-tuple-element.149.refs_0_), channel_id=1, source_target_pairs={{0,16},{4,20},{8,24},{12,28},{16,0},{20,4},{24,8},{28,12},{1,17},{... | collective-permute-start | bytes 774152 | tf_op jit(solution)/shard_map/ppermute | solution.py:110
  200.3 11.7 %collective-permute-start.40 = (bf16[144,896]{1,0:T(8,128)(2,1)S(1)}, bf16[144,896]{1,0:T(8,128)(2,1)S(1)}, u32[]{:S(2)}, u32[]{:S(2)}) collective-permute-start(bf16[144,896]{1,0:T(8,128)(2,1)S(1)} %get-tuple-element.149.refs_0_), channel_id=1, source_target_pairs={{0,24},{4,28},{8,16},{12,20},{16,8},{20,12},{24,0},{28,4},{1,25},{... | collective-permute-start | bytes 774152 | tf_op jit(solution)/shard_map/ppermute | solution.py:110
  (23 other events, 202.3 us)
where the time goes:
time: 228 us; the launch traced here: 223 us
  waiting for transfers between devices  94.5 us (41%)
  Pallas kernels  73.3 us (32%)
  starting transfers between devices  49.4 us (22%)
  local copies, waits for them, and re-layouts  4.13 us (2%)
    ppermute x42, waiting for transfers between devices, swap(): return lax.ppermute(x, axis, pairs)  94.5 us
    pallas_call x28, Pallas kernels, run(): pl.pallas_call(lambda *refs: body(*refs[:n], *refs[n + m:]), out_shape=ou...  73.3 us
    ppermute x42, starting transfers between devices, swap(): return lax.ppermute(x, axis, pairs)  49.4 us
  transfers between devices with their start and end apart: 42, of which 28 were waited for; matrix products, arithmetic and copies ran while one was open for 0% of the time, Pallas kernels for 17%

commit v1 on v0

--- a/solution.py
+++ b/solution.py
@@ -290,17 +290,22 @@
 
 def attention_body(n_space, size, scale, *refs):
     qkv_refs, dattn_refs = refs[:n_space], refs[n_space : 2 * n_space]
-    attn_ref, dqkv_ref, k_ref, v_ref, dk_ref, dv_ref = refs[2 * n_space :]
+    attn_ref, dqkv_ref, q_ref, k_ref, v_ref, do_ref, dk_ref, dv_ref = refs[2 * n_space :]
     rows, group = dattn_refs[0].shape
     heads = group // size
     for b in range(n_space):
         at = slice(b * rows, (b + 1) * rows)
+        q_ref[at, :] = qkv_refs[b][:, :group]
         k_ref[at, :] = qkv_refs[b][:, group : 2 * group]
         v_ref[at, :] = qkv_refs[b][:, 2 * group :]
-    lane_head = iota((rows, group), 1) // size if heads > 1 else None
-    for b in range(n_space):
-        at = slice(b * rows, (b + 1) * rows)
-        queries, d_out = qkv_refs[b][:, :group], dattn_refs[b][...]
+        do_ref[at, :] = dattn_refs[b][...]
+    dk_ref[...] = jnp.zeros(dk_ref.shape, F32)
+    dv_ref[...] = jnp.zeros(dv_ref.shape, F32)
+
+    def step(b, carry):
+        at = pl.ds(pl.multiple_of(b * rows, rows), rows)
+        queries, d_out = q_ref[at, :], do_ref[at, :]
+        lane_head = iota((rows, group), 1) // size if heads > 1 else None
         attn = dq = None
         for h in range(heads):
             if heads > 1:
@@ -317,18 +322,15 @@
             delta = jnp.sum(probs * dprob, axis=-1, keepdims=True)
             dscore = (probs * (dprob - delta)).astype(BF16)
             dq_h = mm(dscore, k_ref[...])
-            dk = mm(dscore, q_h, TN)
-            dv = mm(probs_b, do_h, TN)
-            if b == 0 and h == 0:
-                dk_ref[...] = dk
-                dv_ref[...] = dv
-            else:
-                dk_ref[...] += dk
-                dv_ref[...] += dv
+            dk_ref[...] += mm(dscore, q_h, TN)
+            dv_ref[...] += mm(probs_b, do_h, TN)
             attn = attn_h if attn is None else jnp.where(lane_head == h, attn_h, attn)
             dq = dq_h if dq is None else jnp.where(lane_head == h, dq_h, dq)
         attn_ref[at, :] = attn.astype(BF16)
         dqkv_ref[at, :group] = dq.astype(BF16)
+        return carry
+
+    lax.fori_loop(0, n_space, step, 0, unroll=2)
     dqkv_ref[:, group : 2 * group] = dk_ref[...].astype(BF16)
     dqkv_ref[:, 2 * group :] = dv_ref[...].astype(BF16)
 
@@ -721,7 +723,7 @@
         [struct((positions, group), BF16), struct((positions, 3 * group), BF16)],
         limit=LIMITS["attention"],
         after=[normed_cols[0]],
-        scratch_shapes=[pltpu.VMEM((positions, group), BF16)] * 2 + [pltpu.VMEM((positions, group), F32)] * 2,
+        scratch_shapes=[pltpu.VMEM((positions, group), BF16)] * 4 + [pltpu.VMEM((positions, group), F32)] * 2,
         cost_estimate=cost(6e9, 4e6),
         name="attention",
     )(*qkv_all, *dattn_all)

time: 228 us -> 215 us (0.943); the launches traced: 223 us -> 215 us
  Pallas kernels: 73.3 us -> 65 us
    pallas_call x28, Pallas kernels: 73.3 us -> 65 us  [run(): pl.pallas_call(lambda *refs: body(*refs[:n], *refs[n + m:]), out_shape=ou...]
  transfers between devices with their start and end apart: 42 -> 42, of which waited for: 28 -> 28; matrix products, arithmetic and copies ran while one was open for 0% -> 0% of each run, Pallas kernels for 17% -> 18%
where the time goes in v1:
time: 215 us
  waiting for transfers between devices  94.5 us (44%)
  Pallas kernels  65 us (30%)
  starting transfers between devices  49.4 us (23%)
  local copies, waits for them, and re-layouts  4.13 us (2%)
    ppermute x42, waiting for transfers between devices, swap(): return lax.ppermute(x, axis, pairs)  94.5 us
    pallas_call x28, Pallas kernels, run(): pl.pallas_call(lambda *refs: body(*refs[:n], *refs[n + m:]), out_shape=ou...  65 us
    ppermute x42, starting transfers between devices, swap(): return lax.ppermute(x, axis, pairs)  49.4 us
  transfers between devices with their start and end apart: 42, of which 28 were waited for; matrix products, arithmetic and copies ran while one was open for 0% of the time, Pallas kernels for 18%

profile of v1, /device:TPU:0, one launch (start us, length us, event | category | flops | bytes accessed | tf_op | source)
XLA Modules:
  0.0 214.7 jit_solution(14998639971698182154)
XLA Ops:
  1.3 3.0 %early.1 = (bf16[256,128]{1,0:T(8,128)(2,1)}, bf16[32,1024]{1,0:T(8,128)(2,1)}, bf16[1024,384]{1,0:T(8,128)(2,1)}) custom-call(s32[2]{0:T(128)} %pad_add_fusion.refs_0_, bf16[256,1024]{1,0:T(8,128)(2,1)} %refs_5_.3, bf16[128,1024]{1,0:T(8,128)(2,1)} %refs_2_.4, bf16[1024,384]{1,0:T(8,128)(2,1)} %refs_3_.5), custom_call_target="tpu_custom_call" | custom-call | flops 200000000 | bytes 4000000 | tf_op jit(solution)/shard_map/early/pallas_call | solution.py:84
  4.3 3.0 %collective-permute-start = (bf16[256,128]{1,0:T(8,128)(2,1)}, bf16[256,128]{1,0:T(8,128)(2,1)S(1)}, u32[]{:S(2)}, u32[]{:S(2)}) collective-permute-start(bf16[256,128]{1,0:T(8,128)(2,1)} %get-tuple-element.86.refs_4_), channel_id=1, source_target_pairs={{0,1},{1,0},{2,3},{3,2},{4,5},{5,4},{6,7},{7,6},{8,9},{9,8},{10,11... | collective-permute-start | bytes 196616 | tf_op jit(solution)/shard_map/ppermute | solution.py:110
  7.3 2.6 %collective-permute-start.1 = (bf16[256,128]{1,0:T(8,128)(2,1)}, bf16[256,128]{1,0:T(8,128)(2,1)S(1)}, u32[]{:S(2)}, u32[]{:S(2)}) collective-permute-start(bf16[256,128]{1,0:T(8,128)(2,1)} %get-tuple-element.86.refs_4_), channel_id=1, source_target_pairs={{0,2},{1,3},{2,0},{3,1},{4,6},{5,7},{6,4},{7,5},{8,10},{9,11},{10,... | collective-permute-start | bytes 196616 | tf_op jit(solution)/shard_map/ppermute | solution.py:110
  9.9 2.2 %copy-done = bf16[1024,2048]{1,0:T(8,128)(2,1)S(1)} copy-done((bf16[1024,2048]{1,0:T(8,128)(2,1)S(1)}, bf16[1024,2048]{1,0:T(8,128)(2,1)}, u32[]{:S(2)}) %copy-start) | copy-done | bytes 4194328
  12.1 1.9 copy-done.10
  14.0 8.1 %forward_first.1 = (bf16[3,256,1024]{2,1,0:T(8,128)(2,1)S(1)}, f32[3,256,1024]{2,1,0:T(8,128)S(1)}, f32[3,256,128]{2,1,0:T(8,128)S(1)}, bf16[1024,384]{1,0:T(8,1...) custom-call(bf16[6,256,256]{2,1,0:T(8,128)(2,1)S(1)} %copy-done.3, ...), custom_call_target="tpu_custom_call" | custom-call | flops 6000000000 | bytes 20000000 | tf_op jit(solution)/shard_map/forward_first/pallas_call | solution.py:84
  22.2 4.7 %forward_second.1 = (bf16[3,256,1024]{2,1,0:T(8,128)(2,1)S(1)}, f32[3,256,1024]{2,1,0:T(8,128)S(1)}, f32[3,256,128]{2,1,0:T(8,128)S(1)}, f32[4,32,1152]{2,1,0:T(8,128)S(1)}, f32[4,32,1152]{2,1,0:T(8,128)S(1)}) custom-call(s32[2]{0:T(128)S(1)} %copy-done.6, bf16[6,256,256]{2,1,0:T(8,128)(2,1)S(1)} %copy-done.3, bf16[6,256,1024]{2,1,0:T(8,128)(2,1)S(1)} %copy-done.10, ...), custom_call_target="tpu_custom_call" | custom-call | flops 4000000000 | bytes 10000000 | tf_op jit(solution)/shard_map/forward_second/pallas_call | solution.py:84
  27.0 2.0 collective-permute-done.3.refs_2_
  33.4 2.9 %collective-permute-done.4.refs_1_ = f32[32,1152]{1,0:T(8,128)S(1)} collective-permute-done((f32[32,1152]{1,0:T(8,128)S(1)}, f32[32,1152]{1,0:T(8,128)S(1)}, u32[]{:S(2)}, u32[]{:S(2)}) %collective-permute-start.4) | collective-permute-done | bytes 147488 | tf_op jit(solution)/shard_map/ppermute | solution.py:110
  36.3 4.1 %collective-permute-done.5.refs_2_ = f32[32,1152]{1,0:T(8,128)S(1)} collective-permute-done((f32[32,1152]{1,0:T(8,128)S(1)}, f32[32,1152]{1,0:T(8,128)S(1)}, u32[]{:S(2)}, u32[]{:S(2)}) %collective-permute-start.5) | collective-permute-done | bytes 147488 | tf_op jit(solution)/shard_map/ppermute | solution.py:110
  49.8 2.1 norm.1
  52.7 3.5 %collective-permute-start.12 = (bf16[256,384]{1,0:T(8,128)(2,1)S(1)}, bf16[256,384]{1,0:T(8,128)(2,1)S(1)}, u32[]{:S(2)}, u32[]{:S(2)}) collective-permute-start(bf16[256,384]{1,0:T(8,128)(2,1)S(1)} %get-tuple-element.96.refs_0_), channel_id=1, source_target_pairs={{0,2},{1,3},{2,0},{3,1},{4,6},{5,7},{6,4},{7,5},{8,10},{9,11},{10,... | collective-permute-start | bytes 589832 | tf_op jit(solution)/shard_map/ppermute | solution.py:110
  56.4 6.2 %collective-permute-done.11.refs_2_.refs_1_ = bf16[256,384]{1,0:T(8,128)(2,1)S(1)} collective-permute-done((bf16[256,384]{1,0:T(8,128)(2,1)S(1)}, bf16[256,384]{1,0:T(8,128)(2,1)S(1)}, u32[]{:S(2)}, u32[]{:S(2)}) %collective-permute-start.11) | collective-permute-done | bytes 196640 | tf_op jit(solution)/shard_map/ppermute | solution.py:110
  62.7 7.7 %collective-permute-done.12.refs_3_.refs_2_ = bf16[256,384]{1,0:T(8,128)(2,1)S(1)} collective-permute-done((bf16[256,384]{1,0:T(8,128)(2,1)S(1)}, bf16[256,384]{1,0:T(8,128)(2,1)S(1)}, u32[]{:S(2)}, u32[]{:S(2)}) %collective-permute-start.12) | collective-permute-done | bytes 196640 | tf_op jit(solution)/shard_map/ppermute | solution.py:110
  71.0 4.0 %collective-permute-start.14 = (bf16[256,256]{1,0:T(8,128)(2,1)S(1)}, bf16[256,256]{1,0:T(8,128)(2,1)S(1)}, u32[]{:S(2)}, u32[]{:S(2)}) collective-permute-start(bf16[256,256]{1,0:T(8,128)(2,1)S(1)} %get-tuple-element.100), channel_id=1, source_target_pairs={{0,1},{1,0},{2,3},{3,2},{4,5},{5,4},{6,7},{7,6},{8,9},{9,8},{10,11... | collective-permute-start | bytes 393224 | tf_op jit(solution)/shard_map/ppermute | solution.py:110
  77.5 11.2 %attention.1 = (bf16[1024,128]{1,0:T(8,128)(2,1)S(1)}, bf16[1024,384]{1,0:T(8,128)(2,1)S(1)}) custom-call(bf16[256,384]{1,0:T(8,128)(2,1)S(1)} %get-tuple-element.96.refs_0_, bf16[256,384]{1,0:T(8,128)(2,1)S(1)} %collective-permute-done.11.refs_2_.refs_1_, bf16[256,384]{1,0:T(8,128)(2,1)S(1)} %collective-permute-done.12.refs_3_.refs_2_, ...), custom_call_target="tpu_custom_call" | custom-call | flops 6000000000 | bytes 4000000 | tf_op jit(solution)/shard_map/attention/pallas_call | solution.py:84
  96.3 2.2 %collective-permute-done.19.refs_2_ = bf16[32,1024]{1,0:T(8,128)(2,1)S(1)} collective-permute-done((bf16[32,1024]{1,0:T(8,128)(2,1)S(1)}, bf16[32,1024]{1,0:T(8,128)(2,1)S(1)}, u32[]{:S(2)}, u32[]{:S(2)}) %collective-permute-start.19) | collective-permute-done | bytes 65568 | tf_op jit(solution)/shard_map/ppermute | solution.py:110
  105.1 2.0 collective-permute-done.23
  113.0 2.6 %dvalue.3 = (bf16[3,256,1024]{2,1,0:T(8,128)(2,1)S(1)}, bf16[3,256,256]{2,1,0:T(8,128)(2,1)S(1)}) custom-call(f32[256,1024]{1,0:T(8,128)S(1)} %get-tuple-element.114.refs_0_, f32[3,256,128]{2,1,0:T(8,128)S(1)} %get-tuple-element.115.refs_1_, f32[3,256,1024]{2,1,0:T(8,128)S(1)} %get-tuple-element.127.refs_2_, f32[3,256,128]{2,1,0:T(8,128)S(1)} %get-tuple-element.128.refs_3_), custom_call_target="tpu_custom_call" | custom-call | flops 2000000000 | bytes 5000000 | tf_op jit(solution)/shard_map/dvalue/pallas_call | solution.py:84
  115.6 2.6 %dvalue.2 = (bf16[3,256,1024]{2,1,0:T(8,128)(2,1)S(1)}, bf16[3,256,256]{2,1,0:T(8,128)(2,1)S(1)}) custom-call(f32[256,1024]{1,0:T(8,128)S(1)} %get-tuple-element.114.refs_0_, f32[3,256,128]{2,1,0:T(8,128)S(1)} %get-tuple-element.115.refs_1_, f32[3,256,1024]{2,1,0:T(8,128)S(1)} %get-tuple-element.116.refs_2_, f32[3,256,128]{2,1,0:T(8,128)S(1)} %get-tuple-element.117.refs_3_, ...), custom_call_target="tpu_custom_call" | custom-call | flops 2000000000 | bytes 5000000 | tf_op jit(solution)/shard_map/dvalue/pallas_call | solution.py:84
  118.2 2.4 %collective-permute-done.25.refs_1_.refs_5_ = bf16[2,272,256]{2,1,0:T(8,128)(2,1)S(1)} collective-permute-done((bf16[2,272,256]{2,1,0:T(8,128)(2,1)S(1)}, bf16[2,272,256]{2,1,0:T(8,128)(2,1)S(1)}, u32[]{:S(2)}, u32[]{:S(2)}) %collective-permute-start.25) | collective-permute-done | bytes 278560 | tf_op jit(solution)/shard_map/ppermute | solution.py:110
  120.7 6.1 %value_grad.1 = (bf16[4,128,1152]{2,1,0:T(8,128)(2,1)S(1)}, bf16[4,128,1152]{2,1,0:T(8,128)(2,1)S(1)}) custom-call(s32[2]{0:T(128)S(1)} %copy-done.6, bf16[3,256,1024]{2,1,0:T(8,128)(2,1)S(1)} %get-tuple-element.125.refs_1_, bf16[3,256,1024]{2,1,0:T(8,128)(2,1)S(1)} %get-tuple-element.126.refs_2_, ...), custom_call_target="tpu_custom_call" | custom-call | flops 4000000000 | bytes 10000000 | tf_op jit(solution)/shard_map/value_grad/pallas_call | solution.py:84
  126.8 2.1 collective-permute-start.32
  128.9 4.1 %embed.2 = (bf16[2,784,256]{2,1,0:T(8,128)(2,1)S(1)}, bf16[2,784,256]{2,1,0:T(8,128)(2,1)S(1)}) custom-call(s32[2]{0:T(128)S(1)} %copy-done.6, bf16[3,256,1024]{2,1,0:T(8,128)(2,1)S(1)} %get-tuple-element.122.refs_3_.refs_1_, bf16[3,256,256]{2,1,0:T(8,128)(2,1)S(1)} %get-tuple-element.123.refs_5_.refs_2_, bf16[6,256,256]{2,1,0:T(8,128)(2,1)S(1)} %copy-done.3, ...), custom_call_target="tpu_custom_call" | custom-call | flops 1500000000 | bytes 4000000 | tf_op jit(solution)/shard_map/embed/pallas_call | solution.py:84
  136.9 4.1 %embed.3 = (bf16[2,784,256]{2,1,0:T(8,128)(2,1)S(1)}, bf16[2,784,256]{2,1,0:T(8,128)(2,1)S(1)}) custom-call(s32[2]{0:T(128)S(1)} %copy-done.6, bf16[3,256,1024]{2,1,0:T(8,128)(2,1)S(1)} %get-tuple-element.129.refs_4_.refs_1_, bf16[3,256,256]{2,1,0:T(8,128)(2,1)S(1)} %get-tuple-element.130.refs_6_.refs_2_, bf16[6,256,256]{2,1,0:T(8,128)(2,1)S(1)} %copy-done.3, ...), custom_call_target="tpu_custom_call" | custom-call | flops 1500000000 | bytes 4000000 | tf_op jit(solution)/shard_map/embed/pallas_call | solution.py:84
  144.6 6.4 %collective-permute-done.28.refs_2_ = bf16[128,1152]{1,0:T(8,128)(2,1)S(1)} collective-permute-done((bf16[128,1152]{1,0:T(8,128)(2,1)S(1)}, bf16[128,1152]{1,0:T(8,128)(2,1)S(1)}, u32[]{:S(2)}, u32[]{:S(2)}) %collective-permute-start.28) | collective-permute-done | bytes 294944 | tf_op jit(solution)/shard_map/ppermute | solution.py:110
  151.0 4.5 %collective-permute-done.29.refs_3_ = bf16[128,1152]{1,0:T(8,128)(2,1)S(1)} collective-permute-done((bf16[128,1152]{1,0:T(8,128)(2,1)S(1)}, bf16[128,1152]{1,0:T(8,128)(2,1)S(1)}, u32[]{:S(2)}, u32[]{:S(2)}) %collective-permute-start.29) | collective-permute-done | bytes 294944 | tf_op jit(solution)/shard_map/ppermute | solution.py:110
  163.7 21.1 %collective-permute-done.33.refs_1_.refs_4_ = bf16[2,784,256]{2,1,0:T(8,128)(2,1)S(1)} collective-permute-done((bf16[2,784,256]{2,1,0:T(8,128)(2,1)S(1)}, bf16[2,784,256]{2,1,0:T(8,128)(2,1)S(1)}, u32[]{:S(2)}, u32[]{:S(2)}) %collective-permute-start.33) | collective-permute-done | bytes 802848 | tf_op jit(solution)/shard_map/ppermute | solution.py:110
  189.4 2.5 %collective-permute-start.39 = (bf16[144,896]{1,0:T(8,128)(2,1)S(1)}, bf16[144,896]{1,0:T(8,128)(2,1)S(1)}, u32[]{:S(2)}, u32[]{:S(2)}) collective-permute-start(bf16[144,896]{1,0:T(8,128)(2,1)S(1)} %get-tuple-element.149.refs_0_), channel_id=1, source_target_pairs={{0,16},{4,20},{8,24},{12,28},{16,0},{20,4},{24,8},{28,12},{1,17},{... | collective-permute-start | bytes 774152 | tf_op jit(solution)/shard_map/ppermute | solution.py:110
  192.6 10.1 %collective-permute-done.31.refs_2_.refs_4_ = bf16[784,256]{1,0:T(8,128)(2,1)S(1)} collective-permute-done((bf16[784,256]{1,0:T(8,128)(2,1)S(1)}, bf16[784,256]{1,0:T(8,128)(2,1)S(1)}, u32[]{:S(2)}, u32[]{:S(2)}) %collective-permute-start.31) | collective-permute-done | bytes 401440 | tf_op jit(solution)/shard_map/ppermute | solution.py:110
  203.6 5.6 %collective-permute-done.34.refs_5_ = bf16[784,256]{1,0:T(8,128)(2,1)S(1)} collective-permute-done((bf16[784,256]{1,0:T(8,128)(2,1)S(1)}, bf16[784,256]{1,0:T(8,128)(2,1)S(1)}, u32[]{:S(2)}, u32[]{:S(2)}) %collective-permute-start.34) | collective-permute-done | bytes 401440 | tf_op jit(solution)/shard_map/ppermute | solution.py:110
  212.0 2.8 %final.1 = (f32[1024,512]{1,0:T(8,128)}, f32[1,256]{1,0:T(1,128)}, f32[1024,256]{1,0:T(8,128)}, f32[1,256]{1,0:T(1,128)}) custom-call(s32[2]{0:T(128)S(1)} %copy-done.6, bf16[4,144,896]{2,1,0:T(8,128)(2,1)S(1)} %stack.53.refs_1_, bf16[4,144,896]{2,1,0:T(8,128)(2,1)S(1)} %collective-permute-done.41.refs_2_, f32[1,1024]{1,0:T(1,128)S(1)} %bitcast.19, ...), custom_call_target="tpu_custom_call" | custom-call | flops 200000000 | bytes 5000000 | tf_op jit(solution)/shard_map/final/pallas_call | solution.py:84
  (109 shorter events, 63.3 us)
Async XLA Ops:
  4.3 17.8 %collective-permute-start = (bf16[256,128]{1,0:T(8,128)(2,1)}, bf16[256,128]{1,0:T(8,128)(2,1)S(1)}, u32[]{:S(2)}, u32[]{:S(2)}) collective-permute-start(bf16[256,128]{1,0:T(8,128)(2,1)} %get-tuple-element.86.refs_4_), channel_id=1, source_target_pairs={{0,1},{1,0},{2,3},{3,2},{4,5},{5,4},{6,7},{7,6},{8,9},{9,8},{10,11... | collective-permute-start | bytes 196616 | tf_op jit(solution)/shard_map/ppermute | solution.py:110
  7.3 14.8 %collective-permute-start.1 = (bf16[256,128]{1,0:T(8,128)(2,1)}, bf16[256,128]{1,0:T(8,128)(2,1)S(1)}, u32[]{:S(2)}, u32[]{:S(2)}) collective-permute-start(bf16[256,128]{1,0:T(8,128)(2,1)} %get-tuple-element.86.refs_4_), channel_id=1, source_target_pairs={{0,2},{1,3},{2,0},{3,1},{4,6},{5,7},{6,4},{7,5},{8,10},{9,11},{10,... | collective-permute-start | bytes 196616 | tf_op jit(solution)/shard_map/ppermute | solution.py:110
  9.9 12.2 %collective-permute-start.2 = (bf16[256,128]{1,0:T(8,128)(2,1)}, bf16[256,128]{1,0:T(8,128)(2,1)S(1)}, u32[]{:S(2)}, u32[]{:S(2)}) collective-permute-start(bf16[256,128]{1,0:T(8,128)(2,1)} %get-tuple-element.86.refs_4_), channel_id=1, source_target_pairs={{0,3},{1,2},{2,1},{3,0},{4,7},{5,6},{6,5},{7,4},{8,11},{9,10},{10,... | collective-permute-start | bytes 196616 | tf_op jit(solution)/shard_map/ppermute | solution.py:110
  29.9 6.4 %collective-permute-start.4 = (f32[32,1152]{1,0:T(8,128)S(1)}, f32[32,1152]{1,0:T(8,128)S(1)}, u32[]{:S(2)}, u32[]{:S(2)}) collective-permute-start(f32[32,1152]{1,0:T(8,128)S(1)} %get-tuple-element.90), channel_id=1, source_target_pairs={{0,8},{4,12},{8,0},{12,4},{16,24},{20,28},{24,16},{28,20},{1,9},{5... | collective-permute-start | bytes 442376 | tf_op jit(solution)/shard_map/ppermute | solution.py:110
  31.6 8.8 %collective-permute-start.5 = (f32[32,1152]{1,0:T(8,128)S(1)}, f32[32,1152]{1,0:T(8,128)S(1)}, u32[]{:S(2)}, u32[]{:S(2)}) collective-permute-start(f32[32,1152]{1,0:T(8,128)S(1)} %get-tuple-element.91), channel_id=1, source_target_pairs={{0,16},{4,20},{8,24},{12,28},{16,0},{20,4},{24,8},{28,12},{1,17},{... | collective-permute-start | bytes 442376 | tf_op jit(solution)/shard_map/ppermute | solution.py:110
  33.2 7.3 %collective-permute-start.6 = (f32[32,1152]{1,0:T(8,128)S(1)}, f32[32,1152]{1,0:T(8,128)S(1)}, u32[]{:S(2)}, u32[]{:S(2)}) collective-permute-start(f32[32,1152]{1,0:T(8,128)S(1)} %get-tuple-element.92), channel_id=1, source_target_pairs={{0,24},{4,28},{8,16},{12,20},{16,8},{20,12},{24,0},{28,4},{1,25},{... | collective-permute-start | bytes 442376 | tf_op jit(solution)/shard_map/ppermute | solution.py:110
  42.8 5.3 %collective-permute-start.9 = (bf16[32,1152]{1,0:T(8,128)(2,1)S(1)}, bf16[32,1152]{1,0:T(8,128)(2,1)S(1)}, u32[]{:S(2)}, u32[]{:S(2)}) collective-permute-start(bf16[32,1152]{1,0:T(8,128)(2,1)S(1)} %get-tuple-element.93), channel_id=1, source_target_pairs={{0,24},{4,28},{8,16},{12,20},{16,8},{20,12},{24,0},{28,4},{1,25},{... | collective-permute-start | bytes 221192 | tf_op jit(solution)/shard_map/ppermute | solution.py:110
  52.0 10.7 %collective-permute-start.11 = (bf16[256,384]{1,0:T(8,128)(2,1)S(1)}, bf16[256,384]{1,0:T(8,128)(2,1)S(1)}, u32[]{:S(2)}, u32[]{:S(2)}) collective-permute-start(bf16[256,384]{1,0:T(8,128)(2,1)S(1)} %get-tuple-element.96.refs_0_), channel_id=1, source_target_pairs={{0,1},{1,0},{2,3},{3,2},{4,5},{5,4},{6,7},{7,6},{8,9},{9,8},{10,11... | collective-permute-start | bytes 589832 | tf_op jit(solution)/shard_map/ppermute | solution.py:110
  52.7 17.7 %collective-permute-start.12 = (bf16[256,384]{1,0:T(8,128)(2,1)S(1)}, bf16[256,384]{1,0:T(8,128)(2,1)S(1)}, u32[]{:S(2)}, u32[]{:S(2)}) collective-permute-start(bf16[256,384]{1,0:T(8,128)(2,1)S(1)} %get-tuple-element.96.refs_0_), channel_id=1, source_target_pairs={{0,2},{1,3},{2,0},{3,1},{4,6},{5,7},{6,4},{7,5},{8,10},{9,11},{10,... | collective-permute-start | bytes 589832 | tf_op jit(solution)/shard_map/ppermute | solution.py:110
  56.2 14.2 %collective-permute-start.13 = (bf16[256,384]{1,0:T(8,128)(2,1)S(1)}, bf16[256,384]{1,0:T(8,128)(2,1)S(1)}, u32[]{:S(2)}, u32[]{:S(2)}) collective-permute-start(bf16[256,384]{1,0:T(8,128)(2,1)S(1)} %get-tuple-element.96.refs_0_), channel_id=1, source_target_pairs={{0,3},{1,2},{2,1},{3,0},{4,7},{5,6},{6,5},{7,4},{8,11},{9,10},{10,... | collective-permute-start | bytes 589832 | tf_op jit(solution)/shard_map/ppermute | solution.py:110
  71.0 17.7 %collective-permute-start.14 = (bf16[256,256]{1,0:T(8,128)(2,1)S(1)}, bf16[256,256]{1,0:T(8,128)(2,1)S(1)}, u32[]{:S(2)}, u32[]{:S(2)}) collective-permute-start(bf16[256,256]{1,0:T(8,128)(2,1)S(1)} %get-tuple-element.100), channel_id=1, source_target_pairs={{0,1},{1,0},{2,3},{3,2},{4,5},{5,4},{6,7},{7,6},{8,9},{9,8},{10,11... | collective-permute-start | bytes 393224 | tf_op jit(solution)/shard_map/ppermute | solution.py:110
  75.0 13.7 %collective-permute-start.15 = (bf16[256,256]{1,0:T(8,128)(2,1)S(1)}, bf16[256,256]{1,0:T(8,128)(2,1)S(1)}, u32[]{:S(2)}, u32[]{:S(2)}) collective-permute-start(bf16[256,256]{1,0:T(8,128)(2,1)S(1)} %get-tuple-element.101), channel_id=1, source_target_pairs={{0,2},{1,3},{2,0},{3,1},{4,6},{5,7},{6,4},{7,5},{8,10},{9,11},{10,... | collective-permute-start | bytes 393224 | tf_op jit(solution)/shard_map/ppermute | solution.py:110
  76.1 12.7 %collective-permute-start.16 = (bf16[256,256]{1,0:T(8,128)(2,1)S(1)}, bf16[256,256]{1,0:T(8,128)(2,1)S(1)}, u32[]{:S(2)}, u32[]{:S(2)}) collective-permute-start(bf16[256,256]{1,0:T(8,128)(2,1)S(1)} %get-tuple-element.102), channel_id=1, source_target_pairs={{0,3},{1,2},{2,1},{3,0},{4,7},{5,6},{6,5},{7,4},{8,11},{9,10},{10,... | collective-permute-start | bytes 393224 | tf_op jit(solution)/shard_map/ppermute | solution.py:110
  93.6 5.0 %collective-permute-start.19 = (bf16[32,1024]{1,0:T(8,128)(2,1)S(1)}, bf16[32,1024]{1,0:T(8,128)(2,1)S(1)}, u32[]{:S(2)}, u32[]{:S(2)}) collective-permute-start(bf16[32,1024]{1,0:T(8,128)(2,1)S(1)} %get-tuple-element.107), channel_id=1, source_target_pairs={{0,16},{4,20},{8,24},{12,28},{16,0},{20,4},{24,8},{28,12},{1,17},{... | collective-permute-start | bytes 196616 | tf_op jit(solution)/shard_map/ppermute | solution.py:110
  94.1 5.2 %collective-permute-start.20 = (bf16[32,1024]{1,0:T(8,128)(2,1)S(1)}, bf16[32,1024]{1,0:T(8,128)(2,1)S(1)}, u32[]{:S(2)}, u32[]{:S(2)}) collective-permute-start(bf16[32,1024]{1,0:T(8,128)(2,1)S(1)} %get-tuple-element.108), channel_id=1, source_target_pairs={{0,24},{4,28},{8,16},{12,20},{16,8},{20,12},{24,0},{28,4},{1,25},{... | collective-permute-start | bytes 196616 | tf_op jit(solution)/shard_map/ppermute | solution.py:110
  101.9 5.3 %collective-permute-start.23 = (bf16[32,1152]{1,0:T(8,128)(2,1)S(1)}, bf16[32,1152]{1,0:T(8,128)(2,1)S(1)}, u32[]{:S(2)}, u32[]{:S(2)}) collective-permute-start(bf16[32,1152]{1,0:T(8,128)(2,1)S(1)} %get-tuple-element.113), channel_id=1, source_target_pairs={{0,24},{4,28},{8,16},{12,20},{16,8},{20,12},{24,0},{28,4},{1,25},{... | collective-permute-start | bytes 221192 | tf_op jit(solution)/shard_map/ppermute | solution.py:110
  111.8 8.8 %collective-permute-start.25 = (bf16[2,272,256]{2,1,0:T(8,128)(2,1)S(1)}, bf16[2,272,256]{2,1,0:T(8,128)(2,1)S(1)}, u32[]{:S(2)}, u32[]{:S(2)}) collective-permute-start(bf16[2,272,256]{2,1,0:T(8,128)(2,1)S(1)} %get-tuple-element.131), channel_id=1, source_target_pairs={{0,1},{1,0},{2,3},{3,2},{4,5},{5,4},{6,7},{7,6},{8,9},{9,8},{10,11... | collective-permute-start | bytes 835592 | tf_op jit(solution)/shard_map/ppermute | solution.py:110
  126.7 7.3 %collective-permute-start.27 = (bf16[4,128,1152]{2,1,0:T(8,128)(2,1)S(1)}, bf16[4,128,1152]{2,1,0:T(8,128)(2,1)S(1)}, u32[]{:S(2)}, u32[]{:S(2)}) collective-permute-start(bf16[4,128,1152]{2,1,0:T(8,128)(2,1)S(1)} %get-tuple-element.135), channel_id=1, source_target_pairs={{0,4},{4,0},{8,12},{12,8},{16,20},{20,16},{24,28},{28,24},{1,5},{5... | collective-permute-start | bytes 3538952 | tf_op jit(solution)/shard_map/ppermute | solution.py:110
  126.8 10.1 %collective-permute-start.32 = (bf16[272,256]{1,0:T(8,128)(2,1)S(1)}, bf16[272,256]{1,0:T(8,128)(2,1)S(1)}, u32[]{:S(2)}, u32[]{:S(2)}) collective-permute-start(bf16[272,256]{1,0:T(8,128)(2,1)S(1)} %out_add.1.refs_7_), channel_id=1, source_target_pairs={{0,2},{1,3},{2,0},{3,1},{4,6},{5,7},{6,4},{7,5},{8,10},{9,11},{10,... | collective-permute-start | bytes 417800 | tf_op jit(solution)/shard_map/ppermute | solution.py:110
  133.0 28.8 %collective-permute-start.26 = (bf16[2,784,256]{2,1,0:T(8,128)(2,1)S(1)}, bf16[2,784,256]{2,1,0:T(8,128)(2,1)S(1)}, u32[]{:S(2)}, u32[]{:S(2)}) collective-permute-start(bf16[2,784,256]{2,1,0:T(8,128)(2,1)S(1)} %get-tuple-element.134), channel_id=1, source_target_pairs={{0,1},{1,0},{2,3},{3,2},{4,5},{5,4},{6,7},{7,6},{8,9},{9,8},{10,11... | collective-permute-start | bytes 2408456 | tf_op jit(solution)/shard_map/ppermute | solution.py:110
  141.0 43.8 %collective-permute-start.33 = (bf16[2,784,256]{2,1,0:T(8,128)(2,1)S(1)}, bf16[2,784,256]{2,1,0:T(8,128)(2,1)S(1)}, u32[]{:S(2)}, u32[]{:S(2)}) collective-permute-start(bf16[2,784,256]{2,1,0:T(8,128)(2,1)S(1)} %get-tuple-element.142), channel_id=1, source_target_pairs={{0,1},{1,0},{2,3},{3,2},{4,5},{5,4},{6,7},{7,6},{8,9},{9,8},{10,11... | collective-permute-start | bytes 2408456 | tf_op jit(solution)/shard_map/ppermute | solution.py:110
  141.0 10.0 %collective-permute-start.28 = (bf16[128,1152]{1,0:T(8,128)(2,1)S(1)}, bf16[128,1152]{1,0:T(8,128)(2,1)S(1)}, u32[]{:S(2)}, u32[]{:S(2)}) collective-permute-start(bf16[128,1152]{1,0:T(8,128)(2,1)S(1)} %get-tuple-element.137), channel_id=1, source_target_pairs={{0,8},{4,12},{8,0},{12,4},{16,24},{20,28},{24,16},{28,20},{1,9},{5... | collective-permute-start | bytes 884744 | tf_op jit(solution)/shard_map/ppermute | solution.py:110
  141.9 13.6 %collective-permute-start.29 = (bf16[128,1152]{1,0:T(8,128)(2,1)S(1)}, bf16[128,1152]{1,0:T(8,128)(2,1)S(1)}, u32[]{:S(2)}, u32[]{:S(2)}) collective-permute-start(bf16[128,1152]{1,0:T(8,128)(2,1)S(1)} %get-tuple-element.138), channel_id=1, source_target_pairs={{0,16},{4,20},{8,24},{12,28},{16,0},{20,4},{24,8},{28,12},{1,17},{... | collective-permute-start | bytes 884744 | tf_op jit(solution)/shard_map/ppermute | solution.py:110
  143.4 13.0 %collective-permute-start.30 = (bf16[128,1152]{1,0:T(8,128)(2,1)S(1)}, bf16[128,1152]{1,0:T(8,128)(2,1)S(1)}, u32[]{:S(2)}, u32[]{:S(2)}) collective-permute-start(bf16[128,1152]{1,0:T(8,128)(2,1)S(1)} %get-tuple-element.139), channel_id=1, source_target_pairs={{0,24},{4,28},{8,16},{12,20},{16,8},{20,12},{24,0},{28,4},{1,25},{... | collective-permute-start | bytes 884744 | tf_op jit(solution)/shard_map/ppermute | solution.py:110
  157.3 30.9 %collective-permute-start.35 = (bf16[320,256]{1,0:T(8,128)(2,1)S(1)}, bf16[320,256]{1,0:T(8,128)(2,1)S(1)}, u32[]{:S(2)}, u32[]{:S(2)}) collective-permute-start(bf16[320,256]{1,0:T(8,128)(2,1)S(1)} %get-tuple-element.145), channel_id=1, source_target_pairs={{0,1},{1,0},{2,3},{3,2},{4,5},{5,4},{6,7},{7,6},{8,9},{9,8},{10,11... | collective-permute-start | bytes 491528 | tf_op jit(solution)/shard_map/ppermute | solution.py:110
  159.0 29.1 %collective-permute-start.36 = (bf16[320,256]{1,0:T(8,128)(2,1)S(1)}, bf16[320,256]{1,0:T(8,128)(2,1)S(1)}, u32[]{:S(2)}, u32[]{:S(2)}) collective-permute-start(bf16[320,256]{1,0:T(8,128)(2,1)S(1)} %get-tuple-element.146), channel_id=1, source_target_pairs={{0,2},{1,3},{2,0},{3,1},{4,6},{5,7},{6,4},{7,5},{8,10},{9,11},{10,... | collective-permute-start | bytes 491528 | tf_op jit(solution)/shard_map/ppermute | solution.py:110
  160.4 27.8 %collective-permute-start.37 = (bf16[320,256]{1,0:T(8,128)(2,1)S(1)}, bf16[320,256]{1,0:T(8,128)(2,1)S(1)}, u32[]{:S(2)}, u32[]{:S(2)}) collective-permute-start(bf16[320,256]{1,0:T(8,128)(2,1)S(1)} %get-tuple-element.147), channel_id=1, source_target_pairs={{0,3},{1,2},{2,1},{3,0},{4,7},{5,6},{6,5},{7,4},{8,11},{9,10},{10,... | collective-permute-start | bytes 491528 | tf_op jit(solution)/shard_map/ppermute | solution.py:110
  161.8 40.8 %collective-permute-start.31 = (bf16[784,256]{1,0:T(8,128)(2,1)S(1)}, bf16[784,256]{1,0:T(8,128)(2,1)S(1)}, u32[]{:S(2)}, u32[]{:S(2)}) collective-permute-start(bf16[784,256]{1,0:T(8,128)(2,1)S(1)} %add.4.refs_2_), channel_id=1, source_target_pairs={{0,2},{1,3},{2,0},{3,1},{4,6},{5,7},{6,4},{7,5},{8,10},{9,11},{10,... | collective-permute-start | bytes 1204232 | tf_op jit(solution)/shard_map/ppermute | solution.py:110
  184.8 24.3 %collective-permute-start.34 = (bf16[784,256]{1,0:T(8,128)(2,1)S(1)}, bf16[784,256]{1,0:T(8,128)(2,1)S(1)}, u32[]{:S(2)}, u32[]{:S(2)}) collective-permute-start(bf16[784,256]{1,0:T(8,128)(2,1)S(1)} %add.5.refs_7_), channel_id=1, source_target_pairs={{0,2},{1,3},{2,0},{3,1},{4,6},{5,7},{6,4},{7,5},{8,10},{9,11},{10,... | collective-permute-start | bytes 1204232 | tf_op jit(solution)/shard_map/ppermute | solution.py:110
  189.1 13.6 %collective-permute-start.38 = (bf16[144,896]{1,0:T(8,128)(2,1)S(1)}, bf16[144,896]{1,0:T(8,128)(2,1)S(1)}, u32[]{:S(2)}, u32[]{:S(2)}) collective-permute-start(bf16[144,896]{1,0:T(8,128)(2,1)S(1)} %get-tuple-element.149.refs_0_), channel_id=1, source_target_pairs={{0,8},{4,12},{8,0},{12,4},{16,24},{20,28},{24,16},{28,20},{1,9},{5... | collective-permute-start | bytes 774152 | tf_op jit(solution)/shard_map/ppermute | solution.py:110
  189.4 14.1 %collective-permute-start.39 = (bf16[144,896]{1,0:T(8,128)(2,1)S(1)}, bf16[144,896]{1,0:T(8,128)(2,1)S(1)}, u32[]{:S(2)}, u32[]{:S(2)}) collective-permute-start(bf16[144,896]{1,0:T(8,128)(2,1)S(1)} %get-tuple-element.149.refs_0_), channel_id=1, source_target_pairs={{0,16},{4,20},{8,24},{12,28},{16,0},{20,4},{24,8},{28,12},{1,17},{... | collective-permute-start | bytes 774152 | tf_op jit(solution)/shard_map/ppermute | solution.py:110
  191.9 11.7 %collective-permute-start.40 = (bf16[144,896]{1,0:T(8,128)(2,1)S(1)}, bf16[144,896]{1,0:T(8,128)(2,1)S(1)}, u32[]{:S(2)}, u32[]{:S(2)}) collective-permute-start(bf16[144,896]{1,0:T(8,128)(2,1)S(1)} %get-tuple-element.149.refs_0_), channel_id=1, source_target_pairs={{0,24},{4,28},{8,16},{12,20},{16,8},{20,12},{24,0},{28,4},{1,25},{... | collective-permute-start | bytes 774152 | tf_op jit(solution)/shard_map/ppermute | solution.py:110
  (23 other events, 193.8 us)

commit v2 on v1

--- a/solution.py
+++ b/solution.py
@@ -894,18 +894,19 @@
     kv_parts = [kv_blocks[0]] + [swap(kv_blocks[k], "var", 2 * k) for k in range(1, n_chip)]
     keep1, send1 = embed(half, dv1, dl1, [kv_blocks[0]] + out_parts[2:])
     arrived1 = swap(send1, "space", 1)
+    mine0, sums0 = scatter_embed(keep0, arrived0, [kv_parts[1]])
     part = drows * LANES // cols
     pieces = call(
         functools.partial(packet_split_body, n_chip, n_space),
         [struct((part + 2 * drows, cols), BF16)] * n_space,
         limit=LIMITS["packet_split"],
+        after=sums0,
         in_specs=[SMEM] + [vmem] * n_chip,
         scratch_shapes=[pltpu.VMEM((n_space // 2, drows, kv_cols), BF16)],
         cost_estimate=cost(1e6, 1e6),
         name="packet_split",
     )(me, *kv_parts)
     pieces_all = exchange_direct(pieces, "space")
-    mine0, sums0 = scatter_embed(keep0, arrived0, [pieces[0]])
     mine1, sums1 = scatter_embed(keep1, arrived1, sums0)
     grad_qkv, head_flag = call(
         functools.partial(head_grads_body, n_space),
@@ -919,7 +920,7 @@
         functools.partial(space_sum_body, n_space),
         [struct((drows + 16, kv_cols + LANES + cols), BF16), struct((group, cols), F32)],
         limit=LIMITS["space_sum"],
-        after=sums1 + [head_flag],
+        after=sums1 + mine0[2:] + [head_flag],
         grid=(1,),
         in_specs=[first_slot(x) for x in list(pieces_all) + out_parts],
         cost_estimate=cost(1e6, 1e6),
@@ -930,7 +931,7 @@
         return call(
             stack_body,
             struct((len(parts),) + parts[0].shape, BF16),
-            after=mine0[2:] + mine1[2:],
+            after=mine1[2:],
             cost_estimate=cost(1e6, 1e6),
             name="stack",
         )(*parts)

time: 215 us -> 213 us (level)
  transfers between devices with their start and end apart: 42 -> 42, of which waited for: 28 -> 30; matrix products, arithmetic and copies ran while one was open for 0% -> 0% of each run, Pallas kernels for 18% -> 18%
where the time goes in v2:
time: 213 us
  waiting for transfers between devices  93.4 us (44%)
  Pallas kernels  65 us (31%)
  starting transfers between devices  48.3 us (23%)
  local copies, waits for them, and re-layouts  4.13 us (2%)
    ppermute x42, waiting for transfers between devices, swap(): return lax.ppermute(x, axis, pairs)  93.4 us
    pallas_call x28, Pallas kernels, run(): pl.pallas_call(lambda *refs: body(*refs[:n], *refs[n + m:]), out_shape=ou...  65 us
    ppermute x42, starting transfers between devices, swap(): return lax.ppermute(x, axis, pairs)  48.3 us
  transfers between devices with their start and end apart: 42, of which 30 were waited for; matrix products, arithmetic and copies ran while one was open for 0% of the time, Pallas kernels for 18%

profile of v2, /device:TPU:0, one launch (start us, length us, event | category | flops | bytes accessed | tf_op | source)
XLA Modules:
  0.0 212.5 jit_solution(14978680802098861370)
XLA Ops:
  1.3 3.0 %early.1 = (bf16[256,128]{1,0:T(8,128)(2,1)}, bf16[32,1024]{1,0:T(8,128)(2,1)}, bf16[1024,384]{1,0:T(8,128)(2,1)}) custom-call(s32[2]{0:T(128)} %pad_add_fusion.refs_0_, bf16[256,1024]{1,0:T(8,128)(2,1)} %refs_5_.3, bf16[128,1024]{1,0:T(8,128)(2,1)} %refs_2_.4, bf16[1024,384]{1,0:T(8,128)(2,1)} %refs_3_.5), custom_call_target="tpu_custom_call" | custom-call | flops 200000000 | bytes 4000000 | tf_op jit(solution)/shard_map/early/pallas_call | solution.py:84
  4.3 3.0 %collective-permute-start = (bf16[256,128]{1,0:T(8,128)(2,1)}, bf16[256,128]{1,0:T(8,128)(2,1)S(1)}, u32[]{:S(2)}, u32[]{:S(2)}) collective-permute-start(bf16[256,128]{1,0:T(8,128)(2,1)} %get-tuple-element.86.refs_4_), channel_id=1, source_target_pairs={{0,1},{1,0},{2,3},{3,2},{4,5},{5,4},{6,7},{7,6},{8,9},{9,8},{10,11... | collective-permute-start | bytes 196616 | tf_op jit(solution)/shard_map/ppermute | solution.py:110
  7.3 2.6 %collective-permute-start.1 = (bf16[256,128]{1,0:T(8,128)(2,1)}, bf16[256,128]{1,0:T(8,128)(2,1)S(1)}, u32[]{:S(2)}, u32[]{:S(2)}) collective-permute-start(bf16[256,128]{1,0:T(8,128)(2,1)} %get-tuple-element.86.refs_4_), channel_id=1, source_target_pairs={{0,2},{1,3},{2,0},{3,1},{4,6},{5,7},{6,4},{7,5},{8,10},{9,11},{10,... | collective-permute-start | bytes 196616 | tf_op jit(solution)/shard_map/ppermute | solution.py:110
  9.9 2.2 %copy-done = bf16[1024,2048]{1,0:T(8,128)(2,1)S(1)} copy-done((bf16[1024,2048]{1,0:T(8,128)(2,1)S(1)}, bf16[1024,2048]{1,0:T(8,128)(2,1)}, u32[]{:S(2)}) %copy-start) | copy-done | bytes 4194328
  12.1 1.9 copy-done.10
  14.0 8.1 %forward_first.1 = (bf16[3,256,1024]{2,1,0:T(8,128)(2,1)S(1)}, f32[3,256,1024]{2,1,0:T(8,128)S(1)}, f32[3,256,128]{2,1,0:T(8,128)S(1)}, bf16[1024,384]{1,0:T(8,1...) custom-call(bf16[6,256,256]{2,1,0:T(8,128)(2,1)S(1)} %copy-done.3, ...), custom_call_target="tpu_custom_call" | custom-call | flops 6000000000 | bytes 20000000 | tf_op jit(solution)/shard_map/forward_first/pallas_call | solution.py:84
  22.2 4.7 %forward_second.1 = (bf16[3,256,1024]{2,1,0:T(8,128)(2,1)S(1)}, f32[3,256,1024]{2,1,0:T(8,128)S(1)}, f32[3,256,128]{2,1,0:T(8,128)S(1)}, f32[4,32,1152]{2,1,0:T(8,128)S(1)}, f32[4,32,1152]{2,1,0:T(8,128)S(1)}) custom-call(s32[2]{0:T(128)S(1)} %copy-done.6, bf16[6,256,256]{2,1,0:T(8,128)(2,1)S(1)} %copy-done.3, bf16[6,256,1024]{2,1,0:T(8,128)(2,1)S(1)} %copy-done.10, ...), custom_call_target="tpu_custom_call" | custom-call | flops 4000000000 | bytes 10000000 | tf_op jit(solution)/shard_map/forward_second/pallas_call | solution.py:84
  27.0 2.0 collective-permute-done.3.refs_2_
  33.4 2.9 %collective-permute-done.4.refs_1_ = f32[32,1152]{1,0:T(8,128)S(1)} collective-permute-done((f32[32,1152]{1,0:T(8,128)S(1)}, f32[32,1152]{1,0:T(8,128)S(1)}, u32[]{:S(2)}, u32[]{:S(2)}) %collective-permute-start.4) | collective-permute-done | bytes 147488 | tf_op jit(solution)/shard_map/ppermute | solution.py:110
  36.3 4.1 %collective-permute-done.5.refs_2_ = f32[32,1152]{1,0:T(8,128)S(1)} collective-permute-done((f32[32,1152]{1,0:T(8,128)S(1)}, f32[32,1152]{1,0:T(8,128)S(1)}, u32[]{:S(2)}, u32[]{:S(2)}) %collective-permute-start.5) | collective-permute-done | bytes 147488 | tf_op jit(solution)/shard_map/ppermute | solution.py:110
  49.8 2.1 %norm.1 = (bf16[256,384]{1,0:T(8,128)(2,1)S(1)}, bf16[256,1024]{1,0:T(8,128)(2,1)S(1)}, bf16[256,1152]{1,0:T(8,128)(2,1)S(1)}, f32[32,1024]{1,0:T(8,128)S(1)}, f32[32,128]{1,0:T(8,128)S(1)}) custom-call(s32[2]{0:T(128)S(1)} %copy-done.6, bf16[4,32,1152]{2,1,0:T(8,128)(2,1)S(1)} %pad_maximum_fusion.refs_1_, ...), custom_call_target="tpu_custom_call" | custom-call | flops 800000000 | bytes 5000000 | tf_op jit(solution)/shard_map/norm/pallas_call | solution.py:84
  52.7 3.5 %collective-permute-start.12 = (bf16[256,384]{1,0:T(8,128)(2,1)S(1)}, bf16[256,384]{1,0:T(8,128)(2,1)S(1)}, u32[]{:S(2)}, u32[]{:S(2)}) collective-permute-start(bf16[256,384]{1,0:T(8,128)(2,1)S(1)} %get-tuple-element.96.refs_0_), channel_id=1, source_target_pairs={{0,2},{1,3},{2,0},{3,1},{4,6},{5,7},{6,4},{7,5},{8,10},{9,11},{10,... | collective-permute-start | bytes 589832 | tf_op jit(solution)/shard_map/ppermute | solution.py:110
  56.4 6.2 %collective-permute-done.11.refs_2_.refs_1_ = bf16[256,384]{1,0:T(8,128)(2,1)S(1)} collective-permute-done((bf16[256,384]{1,0:T(8,128)(2,1)S(1)}, bf16[256,384]{1,0:T(8,128)(2,1)S(1)}, u32[]{:S(2)}, u32[]{:S(2)}) %collective-permute-start.11) | collective-permute-done | bytes 196640 | tf_op jit(solution)/shard_map/ppermute | solution.py:110
  62.7 7.7 %collective-permute-done.12.refs_3_.refs_2_ = bf16[256,384]{1,0:T(8,128)(2,1)S(1)} collective-permute-done((bf16[256,384]{1,0:T(8,128)(2,1)S(1)}, bf16[256,384]{1,0:T(8,128)(2,1)S(1)}, u32[]{:S(2)}, u32[]{:S(2)}) %collective-permute-start.12) | collective-permute-done | bytes 196640 | tf_op jit(solution)/shard_map/ppermute | solution.py:110
  71.0 4.0 %collective-permute-start.14 = (bf16[256,256]{1,0:T(8,128)(2,1)S(1)}, bf16[256,256]{1,0:T(8,128)(2,1)S(1)}, u32[]{:S(2)}, u32[]{:S(2)}) collective-permute-start(bf16[256,256]{1,0:T(8,128)(2,1)S(1)} %get-tuple-element.100), channel_id=1, source_target_pairs={{0,1},{1,0},{2,3},{3,2},{4,5},{5,4},{6,7},{7,6},{8,9},{9,8},{10,11... | collective-permute-start | bytes 393224 | tf_op jit(solution)/shard_map/ppermute | solution.py:110
  77.5 11.2 %attention.1 = (bf16[1024,128]{1,0:T(8,128)(2,1)S(1)}, bf16[1024,384]{1,0:T(8,128)(2,1)S(1)}) custom-call(bf16[256,384]{1,0:T(8,128)(2,1)S(1)} %get-tuple-element.96.refs_0_, bf16[256,384]{1,0:T(8,128)(2,1)S(1)} %collective-permute-done.11.refs_2_.refs_1_, bf16[256,384]{1,0:T(8,128)(2,1)S(1)} %collective-permute-done.12.refs_3_.refs_2_, ...), custom_call_target="tpu_custom_call" | custom-call | flops 6000000000 | bytes 4000000 | tf_op jit(solution)/shard_map/attention/pallas_call | solution.py:84
  96.3 2.2 %collective-permute-done.19.refs_2_ = bf16[32,1024]{1,0:T(8,128)(2,1)S(1)} collective-permute-done((bf16[32,1024]{1,0:T(8,128)(2,1)S(1)}, bf16[32,1024]{1,0:T(8,128)(2,1)S(1)}, u32[]{:S(2)}, u32[]{:S(2)}) %collective-permute-start.19) | collective-permute-done | bytes 65568 | tf_op jit(solution)/shard_map/ppermute | solution.py:110
  105.1 2.0 collective-permute-done.23
  113.0 2.6 %dvalue.3 = (bf16[3,256,1024]{2,1,0:T(8,128)(2,1)S(1)}, bf16[3,256,256]{2,1,0:T(8,128)(2,1)S(1)}) custom-call(f32[256,1024]{1,0:T(8,128)S(1)} %get-tuple-element.114.refs_0_, f32[3,256,128]{2,1,0:T(8,128)S(1)} %get-tuple-element.115.refs_1_, f32[3,256,1024]{2,1,0:T(8,128)S(1)} %get-tuple-element.127.refs_2_, f32[3,256,128]{2,1,0:T(8,128)S(1)} %get-tuple-element.128.refs_3_), custom_call_target="tpu_custom_call" | custom-call | flops 2000000000 | bytes 5000000 | tf_op jit(solution)/shard_map/dvalue/pallas_call | solution.py:84
  115.6 2.6 %dvalue.2 = (bf16[3,256,1024]{2,1,0:T(8,128)(2,1)S(1)}, bf16[3,256,256]{2,1,0:T(8,128)(2,1)S(1)}) custom-call(f32[256,1024]{1,0:T(8,128)S(1)} %get-tuple-element.114.refs_0_, f32[3,256,128]{2,1,0:T(8,128)S(1)} %get-tuple-element.115.refs_1_, f32[3,256,1024]{2,1,0:T(8,128)S(1)} %get-tuple-element.116.refs_2_, f32[3,256,128]{2,1,0:T(8,128)S(1)} %get-tuple-element.117.refs_3_, ...), custom_call_target="tpu_custom_call" | custom-call | flops 2000000000 | bytes 5000000 | tf_op jit(solution)/shard_map/dvalue/pallas_call | solution.py:84
  118.2 2.4 %collective-permute-done.25.refs_1_.refs_5_ = bf16[2,272,256]{2,1,0:T(8,128)(2,1)S(1)} collective-permute-done((bf16[2,272,256]{2,1,0:T(8,128)(2,1)S(1)}, bf16[2,272,256]{2,1,0:T(8,128)(2,1)S(1)}, u32[]{:S(2)}, u32[]{:S(2)}) %collective-permute-start.25) | collective-permute-done | bytes 278560 | tf_op jit(solution)/shard_map/ppermute | solution.py:110
  120.7 6.1 %value_grad.1 = (bf16[4,128,1152]{2,1,0:T(8,128)(2,1)S(1)}, bf16[4,128,1152]{2,1,0:T(8,128)(2,1)S(1)}) custom-call(s32[2]{0:T(128)S(1)} %copy-done.6, bf16[3,256,1024]{2,1,0:T(8,128)(2,1)S(1)} %get-tuple-element.125.refs_1_, bf16[3,256,1024]{2,1,0:T(8,128)(2,1)S(1)} %get-tuple-element.126.refs_2_, ...), custom_call_target="tpu_custom_call" | custom-call | flops 4000000000 | bytes 10000000 | tf_op jit(solution)/shard_map/value_grad/pallas_call | solution.py:84
  126.8 2.1 collective-permute-start.30
  128.9 4.1 %embed.2 = (bf16[2,784,256]{2,1,0:T(8,128)(2,1)S(1)}, bf16[2,784,256]{2,1,0:T(8,128)(2,1)S(1)}) custom-call(s32[2]{0:T(128)S(1)} %copy-done.6, bf16[3,256,1024]{2,1,0:T(8,128)(2,1)S(1)} %get-tuple-element.122.refs_3_.refs_1_, bf16[3,256,256]{2,1,0:T(8,128)(2,1)S(1)} %get-tuple-element.123.refs_5_.refs_2_, bf16[6,256,256]{2,1,0:T(8,128)(2,1)S(1)} %copy-done.3, ...), custom_call_target="tpu_custom_call" | custom-call | flops 1500000000 | bytes 4000000 | tf_op jit(solution)/shard_map/embed/pallas_call | solution.py:84
  136.9 4.1 %embed.3 = (bf16[2,784,256]{2,1,0:T(8,128)(2,1)S(1)}, bf16[2,784,256]{2,1,0:T(8,128)(2,1)S(1)}) custom-call(s32[2]{0:T(128)S(1)} %copy-done.6, bf16[3,256,1024]{2,1,0:T(8,128)(2,1)S(1)} %get-tuple-element.129.refs_4_.refs_1_, bf16[3,256,256]{2,1,0:T(8,128)(2,1)S(1)} %get-tuple-element.130.refs_6_.refs_2_, bf16[6,256,256]{2,1,0:T(8,128)(2,1)S(1)} %copy-done.3, ...), custom_call_target="tpu_custom_call" | custom-call | flops 1500000000 | bytes 4000000 | tf_op jit(solution)/shard_map/embed/pallas_call | solution.py:84
  144.6 9.5 %collective-permute-done.26.refs_1_ = bf16[2,784,256]{2,1,0:T(8,128)(2,1)S(1)} collective-permute-done((bf16[2,784,256]{2,1,0:T(8,128)(2,1)S(1)}, bf16[2,784,256]{2,1,0:T(8,128)(2,1)S(1)}, u32[]{:S(2)}, u32[]{:S(2)}) %collective-permute-start.26) | collective-permute-done | bytes 802848 | tf_op jit(solution)/shard_map/ppermute | solution.py:110
  161.8 21.6 %collective-permute-done.31.refs_1_.refs_4_ = bf16[2,784,256]{2,1,0:T(8,128)(2,1)S(1)} collective-permute-done((bf16[2,784,256]{2,1,0:T(8,128)(2,1)S(1)}, bf16[2,784,256]{2,1,0:T(8,128)(2,1)S(1)}, u32[]{:S(2)}, u32[]{:S(2)}) %collective-permute-start.31) | collective-permute-done | bytes 802848 | tf_op jit(solution)/shard_map/ppermute | solution.py:110
  184.1 1.8 head_grads.1
  185.9 4.3 %collective-permute-done.35.refs_1_ = bf16[320,256]{1,0:T(8,128)(2,1)S(1)} collective-permute-done((bf16[320,256]{1,0:T(8,128)(2,1)S(1)}, bf16[320,256]{1,0:T(8,128)(2,1)S(1)}, u32[]{:S(2)}, u32[]{:S(2)}) %collective-permute-start.35) | collective-permute-done | bytes 163872 | tf_op jit(solution)/shard_map/ppermute | solution.py:110
  195.0 5.7 %collective-permute-done.38.refs_1_ = bf16[144,896]{1,0:T(8,128)(2,1)S(1)} collective-permute-done((bf16[144,896]{1,0:T(8,128)(2,1)S(1)}, bf16[144,896]{1,0:T(8,128)(2,1)S(1)}, u32[]{:S(2)}, u32[]{:S(2)}) %collective-permute-start.38) | collective-permute-done | bytes 258080 | tf_op jit(solution)/shard_map/ppermute | solution.py:110
  200.7 3.7 %collective-permute-done.39.refs_2_ = bf16[144,896]{1,0:T(8,128)(2,1)S(1)} collective-permute-done((bf16[144,896]{1,0:T(8,128)(2,1)S(1)}, bf16[144,896]{1,0:T(8,128)(2,1)S(1)}, u32[]{:S(2)}, u32[]{:S(2)}) %collective-permute-start.39) | collective-permute-done | bytes 258080 | tf_op jit(solution)/shard_map/ppermute | solution.py:110
  209.8 2.8 %final.1 = (f32[1024,512]{1,0:T(8,128)}, f32[1,256]{1,0:T(1,128)}, f32[1024,256]{1,0:T(8,128)}, f32[1,256]{1,0:T(1,128)}) custom-call(s32[2]{0:T(128)S(1)} %copy-done.6, bf16[4,144,896]{2,1,0:T(8,128)(2,1)S(1)} %stack.53.refs_1_, bf16[4,144,896]{2,1,0:T(8,128)(2,1)S(1)} %collective-permute-done.41.refs_2_, f32[1,1024]{1,0:T(1,128)S(1)} %bitcast.19, ...), custom_call_target="tpu_custom_call" | custom-call | flops 200000000 | bytes 5000000 | tf_op jit(solution)/shard_map/final/pallas_call | solution.py:84
  (109 shorter events, 64.7 us)
Async XLA Ops:
  4.3 17.8 %collective-permute-start = (bf16[256,128]{1,0:T(8,128)(2,1)}, bf16[256,128]{1,0:T(8,128)(2,1)S(1)}, u32[]{:S(2)}, u32[]{:S(2)}) collective-permute-start(bf16[256,128]{1,0:T(8,128)(2,1)} %get-tuple-element.86.refs_4_), channel_id=1, source_target_pairs={{0,1},{1,0},{2,3},{3,2},{4,5},{5,4},{6,7},{7,6},{8,9},{9,8},{10,11... | collective-permute-start | bytes 196616 | tf_op jit(solution)/shard_map/ppermute | solution.py:110
  7.3 14.8 %collective-permute-start.1 = (bf16[256,128]{1,0:T(8,128)(2,1)}, bf16[256,128]{1,0:T(8,128)(2,1)S(1)}, u32[]{:S(2)}, u32[]{:S(2)}) collective-permute-start(bf16[256,128]{1,0:T(8,128)(2,1)} %get-tuple-element.86.refs_4_), channel_id=1, source_target_pairs={{0,2},{1,3},{2,0},{3,1},{4,6},{5,7},{6,4},{7,5},{8,10},{9,11},{10,... | collective-permute-start | bytes 196616 | tf_op jit(solution)/shard_map/ppermute | solution.py:110
  9.9 12.2 %collective-permute-start.2 = (bf16[256,128]{1,0:T(8,128)(2,1)}, bf16[256,128]{1,0:T(8,128)(2,1)S(1)}, u32[]{:S(2)}, u32[]{:S(2)}) collective-permute-start(bf16[256,128]{1,0:T(8,128)(2,1)} %get-tuple-element.86.refs_4_), channel_id=1, source_target_pairs={{0,3},{1,2},{2,1},{3,0},{4,7},{5,6},{6,5},{7,4},{8,11},{9,10},{10,... | collective-permute-start | bytes 196616 | tf_op jit(solution)/shard_map/ppermute | solution.py:110
  29.9 6.4 %collective-permute-start.4 = (f32[32,1152]{1,0:T(8,128)S(1)}, f32[32,1152]{1,0:T(8,128)S(1)}, u32[]{:S(2)}, u32[]{:S(2)}) collective-permute-start(f32[32,1152]{1,0:T(8,128)S(1)} %get-tuple-element.90), channel_id=1, source_target_pairs={{0,8},{4,12},{8,0},{12,4},{16,24},{20,28},{24,16},{28,20},{1,9},{5... | collective-permute-start | bytes 442376 | tf_op jit(solution)/shard_map/ppermute | solution.py:110
  31.6 8.8 %collective-permute-start.5 = (f32[32,1152]{1,0:T(8,128)S(1)}, f32[32,1152]{1,0:T(8,128)S(1)}, u32[]{:S(2)}, u32[]{:S(2)}) collective-permute-start(f32[32,1152]{1,0:T(8,128)S(1)} %get-tuple-element.91), channel_id=1, source_target_pairs={{0,16},{4,20},{8,24},{12,28},{16,0},{20,4},{24,8},{28,12},{1,17},{... | collective-permute-start | bytes 442376 | tf_op jit(solution)/shard_map/ppermute | solution.py:110
  33.2 7.3 %collective-permute-start.6 = (f32[32,1152]{1,0:T(8,128)S(1)}, f32[32,1152]{1,0:T(8,128)S(1)}, u32[]{:S(2)}, u32[]{:S(2)}) collective-permute-start(f32[32,1152]{1,0:T(8,128)S(1)} %get-tuple-element.92), channel_id=1, source_target_pairs={{0,24},{4,28},{8,16},{12,20},{16,8},{20,12},{24,0},{28,4},{1,25},{... | collective-permute-start | bytes 442376 | tf_op jit(solution)/shard_map/ppermute | solution.py:110
  42.8 5.3 %collective-permute-start.9 = (bf16[32,1152]{1,0:T(8,128)(2,1)S(1)}, bf16[32,1152]{1,0:T(8,128)(2,1)S(1)}, u32[]{:S(2)}, u32[]{:S(2)}) collective-permute-start(bf16[32,1152]{1,0:T(8,128)(2,1)S(1)} %get-tuple-element.93), channel_id=1, source_target_pairs={{0,24},{4,28},{8,16},{12,20},{16,8},{20,12},{24,0},{28,4},{1,25},{... | collective-permute-start | bytes 221192 | tf_op jit(solution)/shard_map/ppermute | solution.py:110
  52.0 10.7 %collective-permute-start.11 = (bf16[256,384]{1,0:T(8,128)(2,1)S(1)}, bf16[256,384]{1,0:T(8,128)(2,1)S(1)}, u32[]{:S(2)}, u32[]{:S(2)}) collective-permute-start(bf16[256,384]{1,0:T(8,128)(2,1)S(1)} %get-tuple-element.96.refs_0_), channel_id=1, source_target_pairs={{0,1},{1,0},{2,3},{3,2},{4,5},{5,4},{6,7},{7,6},{8,9},{9,8},{10,11... | collective-permute-start | bytes 589832 | tf_op jit(solution)/shard_map/ppermute | solution.py:110
  52.7 17.7 %collective-permute-start.12 = (bf16[256,384]{1,0:T(8,128)(2,1)S(1)}, bf16[256,384]{1,0:T(8,128)(2,1)S(1)}, u32[]{:S(2)}, u32[]{:S(2)}) collective-permute-start(bf16[256,384]{1,0:T(8,128)(2,1)S(1)} %get-tuple-element.96.refs_0_), channel_id=1, source_target_pairs={{0,2},{1,3},{2,0},{3,1},{4,6},{5,7},{6,4},{7,5},{8,10},{9,11},{10,... | collective-permute-start | bytes 589832 | tf_op jit(solution)/shard_map/ppermute | solution.py:110
  56.2 14.2 %collective-permute-start.13 = (bf16[256,384]{1,0:T(8,128)(2,1)S(1)}, bf16[256,384]{1,0:T(8,128)(2,1)S(1)}, u32[]{:S(2)}, u32[]{:S(2)}) collective-permute-start(bf16[256,384]{1,0:T(8,128)(2,1)S(1)} %get-tuple-element.96.refs_0_), channel_id=1, source_target_pairs={{0,3},{1,2},{2,1},{3,0},{4,7},{5,6},{6,5},{7,4},{8,11},{9,10},{10,... | collective-permute-start | bytes 589832 | tf_op jit(solution)/shard_map/ppermute | solution.py:110
  71.0 17.7 %collective-permute-start.14 = (bf16[256,256]{1,0:T(8,128)(2,1)S(1)}, bf16[256,256]{1,0:T(8,128)(2,1)S(1)}, u32[]{:S(2)}, u32[]{:S(2)}) collective-permute-start(bf16[256,256]{1,0:T(8,128)(2,1)S(1)} %get-tuple-element.100), channel_id=1, source_target_pairs={{0,1},{1,0},{2,3},{3,2},{4,5},{5,4},{6,7},{7,6},{8,9},{9,8},{10,11... | collective-permute-start | bytes 393224 | tf_op jit(solution)/shard_map/ppermute | solution.py:110
  75.0 13.7 %collective-permute-start.15 = (bf16[256,256]{1,0:T(8,128)(2,1)S(1)}, bf16[256,256]{1,0:T(8,128)(2,1)S(1)}, u32[]{:S(2)}, u32[]{:S(2)}) collective-permute-start(bf16[256,256]{1,0:T(8,128)(2,1)S(1)} %get-tuple-element.101), channel_id=1, source_target_pairs={{0,2},{1,3},{2,0},{3,1},{4,6},{5,7},{6,4},{7,5},{8,10},{9,11},{10,... | collective-permute-start | bytes 393224 | tf_op jit(solution)/shard_map/ppermute | solution.py:110
  76.1 12.7 %collective-permute-start.16 = (bf16[256,256]{1,0:T(8,128)(2,1)S(1)}, bf16[256,256]{1,0:T(8,128)(2,1)S(1)}, u32[]{:S(2)}, u32[]{:S(2)}) collective-permute-start(bf16[256,256]{1,0:T(8,128)(2,1)S(1)} %get-tuple-element.102), channel_id=1, source_target_pairs={{0,3},{1,2},{2,1},{3,0},{4,7},{5,6},{6,5},{7,4},{8,11},{9,10},{10,... | collective-permute-start | bytes 393224 | tf_op jit(solution)/shard_map/ppermute | solution.py:110
  93.6 5.0 %collective-permute-start.19 = (bf16[32,1024]{1,0:T(8,128)(2,1)S(1)}, bf16[32,1024]{1,0:T(8,128)(2,1)S(1)}, u32[]{:S(2)}, u32[]{:S(2)}) collective-permute-start(bf16[32,1024]{1,0:T(8,128)(2,1)S(1)} %get-tuple-element.107), channel_id=1, source_target_pairs={{0,16},{4,20},{8,24},{12,28},{16,0},{20,4},{24,8},{28,12},{1,17},{... | collective-permute-start | bytes 196616 | tf_op jit(solution)/shard_map/ppermute | solution.py:110
  94.1 5.2 %collective-permute-start.20 = (bf16[32,1024]{1,0:T(8,128)(2,1)S(1)}, bf16[32,1024]{1,0:T(8,128)(2,1)S(1)}, u32[]{:S(2)}, u32[]{:S(2)}) collective-permute-start(bf16[32,1024]{1,0:T(8,128)(2,1)S(1)} %get-tuple-element.108), channel_id=1, source_target_pairs={{0,24},{4,28},{8,16},{12,20},{16,8},{20,12},{24,0},{28,4},{1,25},{... | collective-permute-start | bytes 196616 | tf_op jit(solution)/shard_map/ppermute | solution.py:110
  101.9 5.3 %collective-permute-start.23 = (bf16[32,1152]{1,0:T(8,128)(2,1)S(1)}, bf16[32,1152]{1,0:T(8,128)(2,1)S(1)}, u32[]{:S(2)}, u32[]{:S(2)}) collective-permute-start(bf16[32,1152]{1,0:T(8,128)(2,1)S(1)} %get-tuple-element.113), channel_id=1, source_target_pairs={{0,24},{4,28},{8,16},{12,20},{16,8},{20,12},{24,0},{28,4},{1,25},{... | collective-permute-start | bytes 221192 | tf_op jit(solution)/shard_map/ppermute | solution.py:110
  111.8 8.8 %collective-permute-start.25 = (bf16[2,272,256]{2,1,0:T(8,128)(2,1)S(1)}, bf16[2,272,256]{2,1,0:T(8,128)(2,1)S(1)}, u32[]{:S(2)}, u32[]{:S(2)}) collective-permute-start(bf16[2,272,256]{2,1,0:T(8,128)(2,1)S(1)} %get-tuple-element.131), channel_id=1, source_target_pairs={{0,1},{1,0},{2,3},{3,2},{4,5},{5,4},{6,7},{7,6},{8,9},{9,8},{10,11... | collective-permute-start | bytes 835592 | tf_op jit(solution)/shard_map/ppermute | solution.py:110
  126.7 7.3 %collective-permute-start.27 = (bf16[4,128,1152]{2,1,0:T(8,128)(2,1)S(1)}, bf16[4,128,1152]{2,1,0:T(8,128)(2,1)S(1)}, u32[]{:S(2)}, u32[]{:S(2)}) collective-permute-start(bf16[4,128,1152]{2,1,0:T(8,128)(2,1)S(1)} %get-tuple-element.135), channel_id=1, source_target_pairs={{0,4},{4,0},{8,12},{12,8},{16,20},{20,16},{24,28},{28,24},{1,5},{5... | collective-permute-start | bytes 3538952 | tf_op jit(solution)/shard_map/ppermute | solution.py:110
  126.8 10.1 %collective-permute-start.30 = (bf16[272,256]{1,0:T(8,128)(2,1)S(1)}, bf16[272,256]{1,0:T(8,128)(2,1)S(1)}, u32[]{:S(2)}, u32[]{:S(2)}) collective-permute-start(bf16[272,256]{1,0:T(8,128)(2,1)S(1)} %out_add.1.refs_7_), channel_id=1, source_target_pairs={{0,2},{1,3},{2,0},{3,1},{4,6},{5,7},{6,4},{7,5},{8,10},{9,11},{10,... | collective-permute-start | bytes 417800 | tf_op jit(solution)/shard_map/ppermute | solution.py:110
  133.0 21.1 %collective-permute-start.26 = (bf16[2,784,256]{2,1,0:T(8,128)(2,1)S(1)}, bf16[2,784,256]{2,1,0:T(8,128)(2,1)S(1)}, u32[]{:S(2)}, u32[]{:S(2)}) collective-permute-start(bf16[2,784,256]{2,1,0:T(8,128)(2,1)S(1)} %get-tuple-element.134), channel_id=1, source_target_pairs={{0,1},{1,0},{2,3},{3,2},{4,5},{5,4},{6,7},{7,6},{8,9},{9,8},{10,11... | collective-permute-start | bytes 2408456 | tf_op jit(solution)/shard_map/ppermute | solution.py:110
  141.0 42.4 %collective-permute-start.31 = (bf16[2,784,256]{2,1,0:T(8,128)(2,1)S(1)}, bf16[2,784,256]{2,1,0:T(8,128)(2,1)S(1)}, u32[]{:S(2)}, u32[]{:S(2)}) collective-permute-start(bf16[2,784,256]{2,1,0:T(8,128)(2,1)S(1)} %get-tuple-element.139), channel_id=1, source_target_pairs={{0,1},{1,0},{2,3},{3,2},{4,5},{5,4},{6,7},{7,6},{8,9},{9,8},{10,11... | collective-permute-start | bytes 2408456 | tf_op jit(solution)/shard_map/ppermute | solution.py:110
  141.0 13.0 %collective-permute-start.28 = (bf16[128,1152]{1,0:T(8,128)(2,1)S(1)}, bf16[128,1152]{1,0:T(8,128)(2,1)S(1)}, u32[]{:S(2)}, u32[]{:S(2)}) collective-permute-start(bf16[128,1152]{1,0:T(8,128)(2,1)S(1)} %get-tuple-element.136), channel_id=1, source_target_pairs={{0,8},{4,12},{8,0},{12,4},{16,24},{20,28},{24,16},{28,20},{1,9},{5... | collective-permute-start | bytes 884744 | tf_op jit(solution)/shard_map/ppermute | solution.py:110
  141.9 13.6 %collective-permute-start.33 = (bf16[128,1152]{1,0:T(8,128)(2,1)S(1)}, bf16[128,1152]{1,0:T(8,128)(2,1)S(1)}, u32[]{:S(2)}, u32[]{:S(2)}) collective-permute-start(bf16[128,1152]{1,0:T(8,128)(2,1)S(1)} %get-tuple-element.142), channel_id=1, source_target_pairs={{0,16},{4,20},{8,24},{12,28},{16,0},{20,4},{24,8},{28,12},{1,17},{... | collective-permute-start | bytes 884744 | tf_op jit(solution)/shard_map/ppermute | solution.py:110
  143.4 13.0 %collective-permute-start.34 = (bf16[128,1152]{1,0:T(8,128)(2,1)S(1)}, bf16[128,1152]{1,0:T(8,128)(2,1)S(1)}, u32[]{:S(2)}, u32[]{:S(2)}) collective-permute-start(bf16[128,1152]{1,0:T(8,128)(2,1)S(1)} %get-tuple-element.143), channel_id=1, source_target_pairs={{0,24},{4,28},{8,16},{12,20},{16,8},{20,12},{24,0},{28,4},{1,25},{... | collective-permute-start | bytes 884744 | tf_op jit(solution)/shard_map/ppermute | solution.py:110
  154.2 36.5 %collective-permute-start.29 = (bf16[784,256]{1,0:T(8,128)(2,1)S(1)}, bf16[784,256]{1,0:T(8,128)(2,1)S(1)}, u32[]{:S(2)}, u32[]{:S(2)}) collective-permute-start(bf16[784,256]{1,0:T(8,128)(2,1)S(1)} %add.4.refs_2_.refs_5_), channel_id=1, source_target_pairs={{0,2},{1,3},{2,0},{3,1},{4,6},{5,7},{6,4},{7,5},{8,10},{9,11},{10,... | collective-permute-start | bytes 1204232 | tf_op jit(solution)/shard_map/ppermute | solution.py:110
  157.3 32.9 %collective-permute-start.35 = (bf16[320,256]{1,0:T(8,128)(2,1)S(1)}, bf16[320,256]{1,0:T(8,128)(2,1)S(1)}, u32[]{:S(2)}, u32[]{:S(2)}) collective-permute-start(bf16[320,256]{1,0:T(8,128)(2,1)S(1)} %get-tuple-element.145), channel_id=1, source_target_pairs={{0,1},{1,0},{2,3},{3,2},{4,5},{5,4},{6,7},{7,6},{8,9},{9,8},{10,11... | collective-permute-start | bytes 491528 | tf_op jit(solution)/shard_map/ppermute | solution.py:110
  159.0 31.2 %collective-permute-start.36 = (bf16[320,256]{1,0:T(8,128)(2,1)S(1)}, bf16[320,256]{1,0:T(8,128)(2,1)S(1)}, u32[]{:S(2)}, u32[]{:S(2)}) collective-permute-start(bf16[320,256]{1,0:T(8,128)(2,1)S(1)} %get-tuple-element.146), channel_id=1, source_target_pairs={{0,2},{1,3},{2,0},{3,1},{4,6},{5,7},{6,4},{7,5},{8,10},{9,11},{10,... | collective-permute-start | bytes 491528 | tf_op jit(solution)/shard_map/ppermute | solution.py:110
  160.4 30.3 %collective-permute-start.37 = (bf16[320,256]{1,0:T(8,128)(2,1)S(1)}, bf16[320,256]{1,0:T(8,128)(2,1)S(1)}, u32[]{:S(2)}, u32[]{:S(2)}) collective-permute-start(bf16[320,256]{1,0:T(8,128)(2,1)S(1)} %get-tuple-element.147), channel_id=1, source_target_pairs={{0,3},{1,2},{2,1},{3,0},{4,7},{5,6},{6,5},{7,4},{8,11},{9,10},{10,... | collective-permute-start | bytes 491528 | tf_op jit(solution)/shard_map/ppermute | solution.py:110
  183.5 23.5 %collective-permute-start.32 = (bf16[784,256]{1,0:T(8,128)(2,1)S(1)}, bf16[784,256]{1,0:T(8,128)(2,1)S(1)}, u32[]{:S(2)}, u32[]{:S(2)}) collective-permute-start(bf16[784,256]{1,0:T(8,128)(2,1)S(1)} %add.5.refs_7_), channel_id=1, source_target_pairs={{0,2},{1,3},{2,0},{3,1},{4,6},{5,7},{6,4},{7,5},{8,10},{9,11},{10,... | collective-permute-start | bytes 1204232 | tf_op jit(solution)/shard_map/ppermute | solution.py:110
  191.5 9.1 %collective-permute-start.38 = (bf16[144,896]{1,0:T(8,128)(2,1)S(1)}, bf16[144,896]{1,0:T(8,128)(2,1)S(1)}, u32[]{:S(2)}, u32[]{:S(2)}) collective-permute-start(bf16[144,896]{1,0:T(8,128)(2,1)S(1)} %get-tuple-element.149.refs_0_), channel_id=1, source_target_pairs={{0,8},{4,12},{8,0},{12,4},{16,24},{20,28},{24,16},{28,20},{1,9},{5... | collective-permute-start | bytes 774152 | tf_op jit(solution)/shard_map/ppermute | solution.py:110
  192.3 12.0 %collective-permute-start.39 = (bf16[144,896]{1,0:T(8,128)(2,1)S(1)}, bf16[144,896]{1,0:T(8,128)(2,1)S(1)}, u32[]{:S(2)}, u32[]{:S(2)}) collective-permute-start(bf16[144,896]{1,0:T(8,128)(2,1)S(1)} %get-tuple-element.149.refs_0_), channel_id=1, source_target_pairs={{0,16},{4,20},{8,24},{12,28},{16,0},{20,4},{24,8},{28,12},{1,17},{... | collective-permute-start | bytes 774152 | tf_op jit(solution)/shard_map/ppermute | solution.py:110
  193.8 11.4 %collective-permute-start.40 = (bf16[144,896]{1,0:T(8,128)(2,1)S(1)}, bf16[144,896]{1,0:T(8,128)(2,1)S(1)}, u32[]{:S(2)}, u32[]{:S(2)}) collective-permute-start(bf16[144,896]{1,0:T(8,128)(2,1)S(1)} %get-tuple-element.149.refs_0_), channel_id=1, source_target_pairs={{0,24},{4,28},{8,16},{12,20},{16,8},{20,12},{24,0},{28,4},{1,25},{... | collective-permute-start | bytes 774152 | tf_op jit(solution)/shard_map/ppermute | solution.py:110
  (23 other events, 193.8 us)
